TPU v7x, 32 devices: a whole 2x2x4 slice. The times are simulated.
32 devices in a mesh: seq: 32 (over z, y, x, core).
Axes of the slice: x: 2, y: 2, z: 4, core: 2. Of those that a mesh axis runs over, the one named last changes fastest.
Arguments:
- queries: bfloat16 [6144, 1024], P('seq'), may hold values from -200 to 200
- keyval: bfloat16 [2, 6144, 128], P(None, 'seq'), may hold values from -7 to 7
Outputs:
- attended: bfloat16 [6144, 1024], P('seq')
All inputs are finite; a program needn't handle non-finite values.
Results may differ from a plain program's by a relative error of at most 0.0029.
Values may be sent and summed in bfloat16 or wider, within the bound.
No kernel may reach another device: no remote copies, remote signals or barrier semaphores. Data moves between devices by JAX's collectives and lax.ppermute only.
A program may use at most 64 MiB of HBM per device.

v0:
```python
import jax
import jax.numpy as jnp
from jax import lax
from jax.sharding import PartitionSpec as P

QH = 8
KVH = 1
HD = 128


def partner(block, axis, stride):
    count = lax.axis_size(axis)
    route = []
    for low in range(count):
        high = low | 1 << stride
        if high != low and high < count:
            route += [(low, high), (high, low)]
    return lax.ppermute(block, axis, route)


def spread(value, axis, source):
    kept = jnp.where(lax.axis_index(axis) == source, value, 0).astype(value.dtype)
    return lax.psum(kept, axis)


def attend(queries, keyval):
    tok = queries.shape[0]
    total = keyval.shape[1]
    group = QH // KVH
    scale = 1.0 / HD**0.5
    qs = jnp.moveaxis(queries.reshape(tok, KVH, group * HD), 1, 0)
    ks = jnp.moveaxis(keyval[0].reshape(total, KVH, HD), 1, 0)
    vs = jnp.moveaxis(keyval[1].reshape(total, KVH, HD), 1, 0)

    def per_head(items):
        q_group, k_head, v_head = items
        q_group = q_group.reshape(tok, group, HD)
        scores = (
            jnp.einsum("tqd,sd->qts", q_group, k_head, preferred_element_type=jnp.float32) * scale
        )
        top = jnp.max(scores, axis=2, keepdims=True)
        probs = jnp.exp(scores - top)
        totals = jnp.sum(probs, axis=2)
        weights = probs.astype(jnp.bfloat16)
        summed = jnp.einsum("qts,sd->tqd", weights, v_head, preferred_element_type=jnp.float32)
        return summed / jnp.moveaxis(totals, 0, 1)[:, :, None]

    outs = lax.map(per_head, (qs, ks, vs))
    return jnp.moveaxis(outs, 0, 1).reshape(tok, QH * HD).astype(jnp.bfloat16)


def on_device(queries, keyval):
    levels = lax.axis_size("seq").bit_length() - 1
    bit_list = list(range(levels))
    received = {}
    for bit in bit_list:
        received[bit] = partner(keyval, "seq", bit)
    first = spread(keyval, "seq", 0)
    pieces = [keyval] + [received[bit] for bit in range(levels)] + [first]
    gathered = jnp.concatenate(pieces, axis=1)
    return attend(queries, gathered)


def solution(mesh):
    return jax.shard_map(
        on_device,
        mesh=mesh,
        in_specs=(P("seq", None), P(None, "seq", None)),
        out_specs=P("seq", None),
        check_vma=False,
    )
```

profile of v0, /device:TPU:1, one launch (start us, length us, event | category | flops | bytes accessed | tf_op | source)
XLA Modules:
  0.0 148.9 jit_solution(7304933108173020247)
XLA Ops:
  6.5 0.0 copy-start
  6.5 0.0 all-reduce.2.cloned.1.call-start
  6.5 2.1 %collective-permute-start.3 = (bf16[2,192,128]{2,1,0:T(8,128)(2,1)}, bf16[2,192,128]{2,1,0:T(8,128)(2,1)S(1)}, u32[]{:S(2)}, u32[]{:S(2)}) collective-permute-start(bf16[2,192,128]{2,1,0:T(8,128)(2,1)} %param.3), channel_id=1, source_target_pairs={{0,8},{8,0},{1,9},{9,1},{2,10},{10,2},{3,11},{11,3},{4,12},{12,4},... | collective-permute-start | bytes 294920 | tf_op jit(solution)/shard_map/ppermute | solution.py:18
  8.7 1.2 collective-permute-start.2
  9.9 1.2 collective-permute-start.1
  11.1 1.5 %collective-permute-start = (bf16[2,192,128]{2,1,0:T(8,128)(2,1)}, bf16[2,192,128]{2,1,0:T(8,128)(2,1)S(1)}, u32[]{:S(2)}, u32[]{:S(2)}) collective-permute-start(bf16[2,192,128]{2,1,0:T(8,128)(2,1)} %param.3), channel_id=1, source_target_pairs={{0,1},{1,0},{2,3},{3,2},{4,5},{5,4},{6,7},{7,6},{8,9},{9,8},{10,11... | collective-permute-start | bytes 294920 | tf_op jit(solution)/shard_map/ppermute | solution.py:18
  12.6 2.3 %collective-permute-start.4 = (bf16[2,192,128]{2,1,0:T(8,128)(2,1)}, bf16[2,192,128]{2,1,0:T(8,128)(2,1)S(1)}, u32[]{:S(2)}, u32[]{:S(2)}) collective-permute-start(bf16[2,192,128]{2,1,0:T(8,128)(2,1)} %param.3), channel_id=1, source_target_pairs={{0,16},{16,0},{1,17},{17,1},{2,18},{18,2},{3,19},{19,3},{4,20},{20... | collective-permute-start | bytes 294920 | tf_op jit(solution)/shard_map/ppermute | solution.py:18
  14.9 1.6 %broadcast_select_fusion = (bf16[2,192,128]{2,1,0:T(8,128)(2,1)}, bf16[2,1344,128]{2,1,0:T(8,128)(2,1)S(1)}) fusion(bf16[2,192,128]{2,1,0:T(8,128)(2,1)} %param.3, pred[]{:T(512)S(6)} %eq.3), kind=kLoop, calls=%fused_computation.16 | loop fusion | flops 49151 | bytes 294913 | tf_op jit(solution)/shard_map/jit(_where)/select_n | solution.py:22
  16.5 0.0 all-reduce.2.cloned.1.call-update
  16.6 0.0 collective-permute-done
  16.6 0.0 collective-permute-done.1
  16.6 0.0 collective-permute-done.2
  16.7 0.0 collective-permute-done.3
  16.7 3.8 %collective-permute-done.4 = bf16[2,192,128]{2,1,0:T(8,128)(2,1)S(1)} collective-permute-done((bf16[2,192,128]{2,1,0:T(8,128)(2,1)}, bf16[2,192,128]{2,1,0:T(8,128)(2,1)S(1)}, u32[]{:S(2)}, u32[]{:S(2)}) %collective-permute-start.4) | collective-permute-done | bytes 98336 | tf_op jit(solution)/shard_map/ppermute | solution.py:18
  20.5 114.8 %all-reduce.2.cloned.1.call-done = bf16[2,192,128]{2,1,0:T(8,128)(2,1)} async-done(((bf16[2,192,128]{2,1,0:T(8,128)(2,1)}), bf16[2,192,128]{2,1,0:T(8,128)(2,1)}) %all-reduce.2.cloned.1.call-update) | async-done | bytes 98320 | tf_op jit(solution)/shard_map/psum | solution.py:23
  135.3 0.9 constant_dynamic-update-slice_fusion
  136.2 0.0 copy-done
  136.2 1.5 bitcast_reduce_fusion
  137.7 1.8 %fusion.1 = f32[8,192]{1,0:T(8,128)S(1)} fusion(f32[1344,192,8]{0,1,2:T(8,128)S(1)} %get-tuple-element.22, f32[8,192]{1,0:T(8,128)S(1)} %get-tuple-element.20), kind=kLoop, calls=%fused_computation.3 | loop fusion | flops 6191616 | bytes 8269824 | tf_op jit(solution)/shard_map/while/body/eval_jaxpr/reduce_sum | solution.py:43
  139.4 1.8 %fusion.14 = bf16[8,24,8,128]{3,2,1,0:T(8,128)(2,1)S(1)} fusion(f32[1344,192,8]{0,1,2:T(8,128)S(1)} %get-tuple-element.22, f32[8,192]{1,0:T(8,128)S(1)} %get-tuple-element.20, f32[192,8]{0,1:T(8,128)S(1)} %bitcast.51, bf16[2,1344,128]{2,1,0:T(8,128)(2,1)S(1)} %constant_dynamic-update-slice_fusion), kind=kOutput, calls=%fused_computation.9 | convolution fusion | flops 535068672 | bytes 9404416 | tf_op jit(solution)/shard_map/while/body/eval_jaxpr/qts,sd->tqd/dot_general | solution.py:45
  141.2 0.9 copy.15
  (5 shorter events, 0.1 us)
Async XLA Ops:
  6.5 129.7 %copy-start = (bf16[192,1024]{1,0:T(8,128)(2,1)S(1)}, bf16[192,1024]{1,0:T(8,128)(2,1)}, u32[]{:S(2)}) copy-start(bf16[192,1024]{1,0:T(8,128)(2,1)} %param.2) | copy-start | bytes 1179652
  6.5 128.8 %all-reduce.2.cloned.1.call-start = ((), (), s32[]{:S(2)}) async-start(), calls=%async_computation | async-start | bytes 196608 | tf_op jit(solution)/shard_map/psum | solution.py:23
  6.5 10.1 %collective-permute-start.3 = (bf16[2,192,128]{2,1,0:T(8,128)(2,1)}, bf16[2,192,128]{2,1,0:T(8,128)(2,1)S(1)}, u32[]{:S(2)}, u32[]{:S(2)}) collective-permute-start(bf16[2,192,128]{2,1,0:T(8,128)(2,1)} %param.3), channel_id=1, source_target_pairs={{0,8},{8,0},{1,9},{9,1},{2,10},{10,2},{3,11},{11,3},{4,12},{12,4},... | collective-permute-start | bytes 294920 | tf_op jit(solution)/shard_map/ppermute | solution.py:18
  8.7 8.0 %collective-permute-start.2 = (bf16[2,192,128]{2,1,0:T(8,128)(2,1)}, bf16[2,192,128]{2,1,0:T(8,128)(2,1)S(1)}, u32[]{:S(2)}, u32[]{:S(2)}) collective-permute-start(bf16[2,192,128]{2,1,0:T(8,128)(2,1)} %param.3), channel_id=1, source_target_pairs={{0,4},{4,0},{1,5},{5,1},{2,6},{6,2},{3,7},{7,3},{8,12},{12,8},{9,1... | collective-permute-start | bytes 294920 | tf_op jit(solution)/shard_map/ppermute | solution.py:18
  9.9 6.7 %collective-permute-start.1 = (bf16[2,192,128]{2,1,0:T(8,128)(2,1)}, bf16[2,192,128]{2,1,0:T(8,128)(2,1)S(1)}, u32[]{:S(2)}, u32[]{:S(2)}) collective-permute-start(bf16[2,192,128]{2,1,0:T(8,128)(2,1)} %param.3), channel_id=1, source_target_pairs={{0,2},{2,0},{1,3},{3,1},{4,6},{6,4},{5,7},{7,5},{8,10},{10,8},{9,1... | collective-permute-start | bytes 294920 | tf_op jit(solution)/shard_map/ppermute | solution.py:18
  11.1 5.4 %collective-permute-start = (bf16[2,192,128]{2,1,0:T(8,128)(2,1)}, bf16[2,192,128]{2,1,0:T(8,128)(2,1)S(1)}, u32[]{:S(2)}, u32[]{:S(2)}) collective-permute-start(bf16[2,192,128]{2,1,0:T(8,128)(2,1)} %param.3), channel_id=1, source_target_pairs={{0,1},{1,0},{2,3},{3,2},{4,5},{5,4},{6,7},{7,6},{8,9},{9,8},{10,11... | collective-permute-start | bytes 294920 | tf_op jit(solution)/shard_map/ppermute | solution.py:18
  12.6 7.9 %collective-permute-start.4 = (bf16[2,192,128]{2,1,0:T(8,128)(2,1)}, bf16[2,192,128]{2,1,0:T(8,128)(2,1)S(1)}, u32[]{:S(2)}, u32[]{:S(2)}) collective-permute-start(bf16[2,192,128]{2,1,0:T(8,128)(2,1)} %param.3), channel_id=1, source_target_pairs={{0,16},{16,0},{1,17},{17,1},{2,18},{18,2},{3,19},{19,3},{4,20},{20... | collective-permute-start | bytes 294920 | tf_op jit(solution)/shard_map/ppermute | solution.py:18
Sparse Core Ops, SparseCore 0:
  16.7 118.5 all-reduce.1
where the time goes:
time: 150 us; the launch traced here: 149 us
  waiting for transfers between devices  119 us (79%)
  between operations  13.5 us (9%)
  starting transfers between devices  8.4 us (6%)
  other arithmetic  3.35 us (2%)
  matrix products  3.26 us (2%)
  local copies, waits for them, and re-layouts  1.85 us (1%)
    psum x1, waiting for transfers between devices, spread(): return lax.psum(kept, axis)  115 us
    ppermute x5, starting transfers between devices, partner(): return lax.ppermute(block, axis, route)  8.4 us
    ppermute x5, waiting for transfers between devices, partner(): return lax.ppermute(block, axis, route)  3.82 us
  transfers between devices with their start and end apart: 6, of which 2 were waited for; matrix products, arithmetic and copies ran while one was open for 1% of the time, Pallas kernels for 0%

commit v1 on v0

v1 whole, which is shorter than its diff:
```python
import functools
import math

import jax
import jax.numpy as jnp
from jax import lax
from jax.experimental import pallas as pl
from jax.experimental.pallas import tpu as pltpu
from jax.sharding import PartitionSpec as P

HD = 128
AXIS = "seq"
FANOUT = 2
PAIR = 2
LOG2E = math.log2(math.e)
VMEM = pl.BlockSpec(memory_space=pltpu.VMEM)


def hops(a, b):
    return (a ^ b).bit_count()


def fill(real, count):
    goes = dict(real)
    open_to = set(range(count)) - set(goes.values())
    late = []
    for i in range(count):
        if i in goes:
            continue
        if i ^ 1 in open_to:
            goes[i] = i ^ 1
            open_to.remove(i ^ 1)
        else:
            late.append(i)
    for i in late:
        goes[i] = min(sorted(open_to), key=lambda t: (t == i, hops(t, i), t))
        open_to.remove(goes[i])
    for i in range(count):
        if goes[i] == i:
            goes[i], goes[i ^ 1] = goes[i ^ 1], goes[i]
    return sorted(goes.items())


def plan(informed, count):
    informed = set(informed)
    missing = [t for t in range(0, count, 2) if t not in informed]
    waves = []
    while missing:
        sends = {s: [] for s in sorted(informed) if s}
        order = sorted(missing, key=lambda t: (-min(hops(s, t) for s in sends), -t))
        for t in order:
            free = [s for s in sends if len(sends[s]) < FANOUT]
            if not free:
                break
            s = min(free, key=lambda s: (hops(s, t), len(sends[s]), -s))
            sends[s].append(t)
        wave = [[(s, ts[k]) for s, ts in sends.items() if len(ts) > k] for k in range(FANOUT)]
        wave = [w for w in wave if w]
        waves.append(wave)
        reached = {t for w in wave for _, t in w}
        informed |= reached
        missing = [t for t in missing if t not in reached]
    return waves


def member(me, devices):
    hit = me == devices[0]
    for d in devices[1:]:
        hit = hit | (me == d)
    return hit


def attend_body(blocks, first, last, *refs):
    it = iter(refs)
    q_ref = next(it)
    kv = [next(it) for _ in range(blocks)]
    if not first:
        m_in, l_in, a_in = next(it), next(it), next(it)
    if last:
        o_ref = next(it)
    else:
        m_out, l_out, a_out = next(it), next(it), next(it)
    tok, width = q_ref.shape
    heads = width // HD
    group = math.gcd(heads, PAIR)
    keys = [r[0] for r in kv]
    vals = [r[1].T for r in kv]
    keys = keys[0] if blocks == 1 else jnp.concatenate(keys, axis=0)
    vals = vals[0] if blocks == 1 else jnp.concatenate(vals, axis=1)
    for g in range(0, heads, group):
        q = jnp.concatenate([q_ref[:, pl.ds(h * HD, HD)] for h in range(g, g + group)], axis=0)
        cols = pl.ds(g * tok, group * tok)
        s = lax.dot_general(keys, q, (((1,), (1,)), ((), ())), preferred_element_type=jnp.float32)
        s = s * (LOG2E / math.sqrt(HD))
        top = jnp.max(s, axis=0, keepdims=True)
        if not first:
            old = m_in[:, cols]
            top = jnp.maximum(old, top)
            alpha = jnp.exp2(old - top)
        p = jnp.exp2(s - top)
        total = jnp.sum(p, axis=0, keepdims=True)
        out = jnp.dot(vals, p.astype(jnp.bfloat16), preferred_element_type=jnp.float32)
        if not first:
            total = total + alpha * l_in[:, cols]
            out = out + alpha * a_in[:, cols]
        if last:
            out = (out / total).T.astype(o_ref.dtype)
            for h in range(group):
                o_ref[:, pl.ds((g + h) * HD, HD)] = out[h * tok : (h + 1) * tok]
        else:
            m_out[:, cols] = top
            l_out[:, cols] = total
            a_out[:, cols] = out


def attend(queries, blocks, state=None, last=False):
    tok, width = queries.shape
    rows = width // HD * tok
    if last:
        out_shape, out_specs = jax.ShapeDtypeStruct((tok, width), queries.dtype), VMEM
    else:
        out_shape = tuple(pltpu.VMEM((n, rows), jnp.float32) for n in (1, 1, HD))
        out_specs = (VMEM,) * 3
    args = [queries, *blocks, *(state or ())]
    args = [pltpu.with_memory_space_constraint(a, pltpu.VMEM) for a in args]
    pairs = rows * sum(b.shape[1] for b in blocks)
    return pl.pallas_call(
        functools.partial(attend_body, len(blocks), state is None, last),
        out_shape=out_shape,
        in_specs=[VMEM] * len(args),
        out_specs=out_specs,
        compiler_params=pltpu.CompilerParams(vmem_limit_bytes=24 << 20),
        cost_estimate=pl.CostEstimate(flops=4 * pairs * HD, bytes_accessed=0, transcendentals=pairs),
    )(*args)


def on_device(queries, keyval):
    count = lax.axis_size(AXIS)
    levels = count.bit_length() - 1
    me = lax.axis_index(AXIS)
    far = 3 << levels - 2

    def swap(value, bit):
        return lax.ppermute(value, AXIS, [(i, i ^ 1 << bit) for i in range(count)])

    def send(value, real):
        return lax.ppermute(value, AXIS, fill(real, count))

    received = {}
    first = None
    informed = [0, 1]
    for bit in [*range(levels - 1, max(levels - 3, 0), -1), None, *range(max(levels - 3, 0), 0, -1)]:
        if bit is None:
            got, holder = send(keyval, [(0, far)]), far
        else:
            got, holder = swap(keyval, bit), 1 << bit
            received[bit] = got
        informed.append(holder)
        first = got if first is None else jnp.where(me == holder, got, first)
    state = attend(queries, [keyval])
    for wave in plan(informed, count):
        came = [(send(first, real), [t for _, t in real]) for real in wave]
        for got, holders in came:
            first = jnp.where(member(me, holders), got, first)
    state = attend(queries, [received[bit] for bit in range(1, levels)], state)
    first = jnp.where(me == 0, keyval, first)
    both = swap(jnp.concatenate([keyval, first], axis=0), 0)
    first = jnp.where(me % 2 == 1, both[2:], first)
    return attend(queries, [both[:2], first], state, last=True)


def solution(mesh):
    return jax.shard_map(
        on_device,
        mesh=mesh,
        in_specs=(P(AXIS, None), P(None, AXIS, None)),
        out_specs=P(AXIS, None),
        check_vma=False,
    )
```

time: 150 us -> 22.8 us (0.15)
  the two profiles are of different devices: /device:TPU:1 before, /device:TPU:11 now
where the time goes in v1:
time: 22.8 us; the launch traced here: 22.7 us
  starting transfers between devices  10.5 us (46%)
  Pallas kernels  6.36 us (28%)
  waiting for transfers between devices  5.7 us (25%)
    ppermute x5, starting transfers between devices, swap(): return lax.ppermute(value, AXIS, [(i, i ^ 1 << bit) for i in range(count)])  7.81 us
    pallas_call x3, Pallas kernels, attend(): pl.pallas_call(functools.partial(attend_body, len(blocks), state is None,...  6.36 us
    ppermute x5, waiting for transfers between devices, swap(): return lax.ppermute(value, AXIS, [(i, i ^ 1 << bit) for i in range(count)])  4.06 us
    ppermute x3, starting transfers between devices, send(): return lax.ppermute(value, AXIS, fill(real, count))  2.65 us
    ppermute x3, waiting for transfers between devices, send(): return lax.ppermute(value, AXIS, fill(real, count))  1.64 us
  transfers between devices with their start and end apart: 8, of which 6 were waited for; matrix products, arithmetic and copies ran while one was open for 0% of the time, Pallas kernels for 17%

profile of v1, /device:TPU:11, one launch (start us, length us, event | category | flops | bytes accessed | tf_op | source)
XLA Modules:
  0.0 22.7 jit_solution(11348552659772705436)
XLA Ops:
  0.0 2.3 %collective-permute-start.4 = (bf16[2,192,128]{2,1,0:T(8,128)(2,1)}, bf16[2,192,128]{2,1,0:T(8,128)(2,1)S(1)}, u32[]{:S(2)}, u32[]{:S(2)}) collective-permute-start(bf16[2,192,128]{2,1,0:T(8,128)(2,1)} %refs_1_.1), channel_id=1, source_target_pairs={{0,16},{1,17},{2,18},{3,19},{4,20},{5,21},{6,22},{7,23},{8,24},{9,... | collective-permute-start | bytes 294920 | tf_op jit(solution)/shard_map/ppermute | solution.py:144
  2.3 0.2 collective-permute-start.3
  2.5 1.2 %collective-permute-start.2 = (bf16[2,192,128]{2,1,0:T(8,128)(2,1)}, bf16[2,192,128]{2,1,0:T(8,128)(2,1)S(1)}, u32[]{:S(2)}, u32[]{:S(2)}) collective-permute-start(bf16[2,192,128]{2,1,0:T(8,128)(2,1)} %refs_1_.1), channel_id=1, source_target_pairs={{0,24},{1,0},{2,3},{3,2},{4,5},{5,4},{6,7},{7,6},{8,9},{9,8},{10,1... | collective-permute-start | bytes 294920 | tf_op jit(solution)/shard_map/ppermute | solution.py:147
  3.7 1.2 %collective-permute-start.1 = (bf16[2,192,128]{2,1,0:T(8,128)(2,1)}, bf16[2,192,128]{2,1,0:T(8,128)(2,1)S(1)}, u32[]{:S(2)}, u32[]{:S(2)}) collective-permute-start(bf16[2,192,128]{2,1,0:T(8,128)(2,1)} %refs_1_.1), channel_id=1, source_target_pairs={{0,4},{1,5},{2,6},{3,7},{4,0},{5,1},{6,2},{7,3},{8,12},{9,13},{10,... | collective-permute-start | bytes 294920 | tf_op jit(solution)/shard_map/ppermute | solution.py:144
  5.0 0.3 %collective-permute-start = (bf16[2,192,128]{2,1,0:T(8,128)(2,1)}, bf16[2,192,128]{2,1,0:T(8,128)(2,1)S(1)}, u32[]{:S(2)}, u32[]{:S(2)}) collective-permute-start(bf16[2,192,128]{2,1,0:T(8,128)(2,1)} %refs_1_.1), channel_id=1, source_target_pairs={{0,2},{1,3},{2,0},{3,1},{4,6},{5,7},{6,4},{7,5},{8,10},{9,11},{10,... | collective-permute-start | bytes 294920 | tf_op jit(solution)/shard_map/ppermute | solution.py:144
  5.2 1.9 %collective-permute-done.4.refs_4_ = bf16[2,192,128]{2,1,0:T(8,128)(2,1)S(1)} collective-permute-done((bf16[2,192,128]{2,1,0:T(8,128)(2,1)}, bf16[2,192,128]{2,1,0:T(8,128)(2,1)S(1)}, u32[]{:S(2)}, u32[]{:S(2)}) %collective-permute-start.4) | collective-permute-done | bytes 98336 | tf_op jit(solution)/shard_map/ppermute | solution.py:144
  7.1 0.2 collective-permute-done.3.refs_3_
  7.3 0.0 collective-permute-done.2
  7.3 1.0 %collective-permute-done.1.refs_2_ = bf16[2,192,128]{2,1,0:T(8,128)(2,1)S(1)} collective-permute-done((bf16[2,192,128]{2,1,0:T(8,128)(2,1)}, bf16[2,192,128]{2,1,0:T(8,128)(2,1)S(1)}, u32[]{:S(2)}, u32[]{:S(2)}) %collective-permute-start.1) | collective-permute-done | bytes 98336 | tf_op jit(solution)/shard_map/ppermute | solution.py:144
  8.4 0.9 %collective-permute-done.refs_1_ = bf16[2,192,128]{2,1,0:T(8,128)(2,1)S(1)} collective-permute-done((bf16[2,192,128]{2,1,0:T(8,128)(2,1)}, bf16[2,192,128]{2,1,0:T(8,128)(2,1)S(1)}, u32[]{:S(2)}, u32[]{:S(2)}) %collective-permute-start) | collective-permute-done | bytes 98336 | tf_op jit(solution)/shard_map/ppermute | solution.py:144
  9.3 0.0 copy-start.1
  9.3 1.2 %collective-permute-start.6 = (bf16[2,192,128]{2,1,0:T(8,128)(2,1)S(1)}, bf16[2,192,128]{2,1,0:T(8,128)(2,1)S(1)}, u32[]{:S(2)}, u32[]{:S(2)}) collective-permute-start(bf16[2,192,128]{2,1,0:T(8,128)(2,1)S(1)} %select_select_fusion.1), channel_id=1, source_target_pairs={{0,1},{1,0},{2,26},{3,2},{4,20},{5,4},{6,7},{7,6},{8,14},{9,8},{10... | collective-permute-start | bytes 294920 | tf_op jit(solution)/shard_map/ppermute | solution.py:147
  10.5 0.3 %collective-permute-start.5 = (bf16[2,192,128]{2,1,0:T(8,128)(2,1)S(1)}, bf16[2,192,128]{2,1,0:T(8,128)(2,1)S(1)}, u32[]{:S(2)}, u32[]{:S(2)}) collective-permute-start(bf16[2,192,128]{2,1,0:T(8,128)(2,1)S(1)} %select_select_fusion.1), channel_id=1, source_target_pairs={{0,1},{1,0},{2,10},{3,2},{4,6},{5,4},{6,7},{7,3},{8,12},{9,8},{10,... | collective-permute-start | bytes 294920 | tf_op jit(solution)/shard_map/ppermute | solution.py:147
  10.7 0.0 copy-start
  10.7 0.7 %collective-permute-done.6 = bf16[2,192,128]{2,1,0:T(8,128)(2,1)S(1)} collective-permute-done((bf16[2,192,128]{2,1,0:T(8,128)(2,1)S(1)}, bf16[2,192,128]{2,1,0:T(8,128)(2,1)S(1)}, u32[]{:S(2)}, u32[]{:S(2)}) %collective-permute-start.6) | collective-permute-done | bytes 98336 | tf_op jit(solution)/shard_map/ppermute | solution.py:147
  11.4 1.0 %collective-permute-done.5 = bf16[2,192,128]{2,1,0:T(8,128)(2,1)S(1)} collective-permute-done((bf16[2,192,128]{2,1,0:T(8,128)(2,1)S(1)}, bf16[2,192,128]{2,1,0:T(8,128)(2,1)S(1)}, u32[]{:S(2)}, u32[]{:S(2)}) %collective-permute-start.5) | collective-permute-done | bytes 98336 | tf_op jit(solution)/shard_map/ppermute | solution.py:147
  12.4 0.0 copy-done.1
  12.4 3.8 %collective-permute-start.7 = (bf16[4,192,128]{2,1,0:T(8,128)(2,1)S(1)}, bf16[4,192,128]{2,1,0:T(8,128)(2,1)S(1)}, u32[]{:S(2)}, u32[]{:S(2)}) collective-permute-start(bf16[4,192,128]{2,1,0:T(8,128)(2,1)S(1)} %pad_maximum_fusion), channel_id=1, source_target_pairs={{0,1},{1,0},{2,3},{3,2},{4,5},{5,4},{6,7},{7,6},{8,9},{9,8},{10,11... | collective-permute-start | bytes 589832 | tf_op jit(solution)/shard_map/ppermute | solution.py:144
  16.3 0.0 copy-done
  16.3 1.2 %shard_map.28 = (f32[1,1536]{1,0:T(1,128)S(1)}, f32[1,1536]{1,0:T(1,128)S(1)}, f32[128,1536]{1,0:T(8,128)S(1)}) custom-call(bf16[192,1024]{1,0:T(8,128)(2,1)S(1)} %copy-done, bf16[2,192,128]{2,1,0:T(8,128)(2,1)S(1)} %copy-done.1), custom_call_target="tpu_custom_call" | custom-call | flops 150994944 | tf_op jit(solution)/shard_map/pallas_call | solution.py:127
  17.5 2.6 %shard_map.29 = (f32[1,1536]{1,0:T(1,128)S(1)}, f32[1,1536]{1,0:T(1,128)S(1)}, f32[128,1536]{1,0:T(8,128)S(1)}) custom-call(bf16[192,1024]{1,0:T(8,128)(2,1)S(1)} %copy-done, bf16[2,192,128]{2,1,0:T(8,128)(2,1)S(1)} %collective-permute-done.refs_1_, bf16[2,192,128]{2,1,0:T(8,128)(2,1)S(1)} %collective-permute-done.1.refs_2_, ...), custom_call_target="tpu_custom_call" | custom-call | flops 603979776 | tf_op jit(solution)/shard_map/pallas_call | solution.py:127
  20.1 0.0 collective-permute-done.7
  20.1 2.5 %shard_map.30 = bf16[192,1024]{1,0:T(8,128)(2,1)} custom-call(bf16[192,1024]{1,0:T(8,128)(2,1)S(1)} %copy-done, bf16[2,192,128]{2,1,0:T(8,128)(2,1)S(1)} %get-tuple-element.18.refs_1_, bf16[2,192,128]{2,1,0:T(8,128)(2,1)S(1)} %get-tuple-element.17.refs_2_, f32[1,1536]{1,0:T(1,128)S(1)} %get-tuple-element.14.refs_3_, ...), custom_call_target="tpu_custom_call" | custom-call | flops 301989888 | tf_op jit(solution)/shard_map/pallas_call | solution.py:127
  (4 shorter events, 0.1 us)
Async XLA Ops:
  0.0 7.1 %collective-permute-start.4 = (bf16[2,192,128]{2,1,0:T(8,128)(2,1)}, bf16[2,192,128]{2,1,0:T(8,128)(2,1)S(1)}, u32[]{:S(2)}, u32[]{:S(2)}) collective-permute-start(bf16[2,192,128]{2,1,0:T(8,128)(2,1)} %refs_1_.1), channel_id=1, source_target_pairs={{0,16},{1,17},{2,18},{3,19},{4,20},{5,21},{6,22},{7,23},{8,24},{9,... | collective-permute-start | bytes 294920 | tf_op jit(solution)/shard_map/ppermute | solution.py:144
  2.3 5.0 %collective-permute-start.3 = (bf16[2,192,128]{2,1,0:T(8,128)(2,1)}, bf16[2,192,128]{2,1,0:T(8,128)(2,1)S(1)}, u32[]{:S(2)}, u32[]{:S(2)}) collective-permute-start(bf16[2,192,128]{2,1,0:T(8,128)(2,1)} %refs_1_.1), channel_id=1, source_target_pairs={{0,8},{1,9},{2,10},{3,11},{4,12},{5,13},{6,14},{7,15},{8,0},{9,1},... | collective-permute-start | bytes 294920 | tf_op jit(solution)/shard_map/ppermute | solution.py:144
  2.5 4.9 %collective-permute-start.2 = (bf16[2,192,128]{2,1,0:T(8,128)(2,1)}, bf16[2,192,128]{2,1,0:T(8,128)(2,1)S(1)}, u32[]{:S(2)}, u32[]{:S(2)}) collective-permute-start(bf16[2,192,128]{2,1,0:T(8,128)(2,1)} %refs_1_.1), channel_id=1, source_target_pairs={{0,24},{1,0},{2,3},{3,2},{4,5},{5,4},{6,7},{7,6},{8,9},{9,8},{10,1... | collective-permute-start | bytes 294920 | tf_op jit(solution)/shard_map/ppermute | solution.py:147
  3.7 4.6 %collective-permute-start.1 = (bf16[2,192,128]{2,1,0:T(8,128)(2,1)}, bf16[2,192,128]{2,1,0:T(8,128)(2,1)S(1)}, u32[]{:S(2)}, u32[]{:S(2)}) collective-permute-start(bf16[2,192,128]{2,1,0:T(8,128)(2,1)} %refs_1_.1), channel_id=1, source_target_pairs={{0,4},{1,5},{2,6},{3,7},{4,0},{5,1},{6,2},{7,3},{8,12},{9,13},{10,... | collective-permute-start | bytes 294920 | tf_op jit(solution)/shard_map/ppermute | solution.py:144
  5.0 4.3 %collective-permute-start = (bf16[2,192,128]{2,1,0:T(8,128)(2,1)}, bf16[2,192,128]{2,1,0:T(8,128)(2,1)S(1)}, u32[]{:S(2)}, u32[]{:S(2)}) collective-permute-start(bf16[2,192,128]{2,1,0:T(8,128)(2,1)} %refs_1_.1), channel_id=1, source_target_pairs={{0,2},{1,3},{2,0},{3,1},{4,6},{5,7},{6,4},{7,5},{8,10},{9,11},{10,... | collective-permute-start | bytes 294920 | tf_op jit(solution)/shard_map/ppermute | solution.py:144
  9.3 3.1 %copy-start.1 = (bf16[2,192,128]{2,1,0:T(8,128)(2,1)S(1)}, bf16[2,192,128]{2,1,0:T(8,128)(2,1)}, u32[]{:S(2)}) copy-start(bf16[2,192,128]{2,1,0:T(8,128)(2,1)} %refs_1_.1) | copy-start | bytes 294916
  9.3 2.1 %collective-permute-start.6 = (bf16[2,192,128]{2,1,0:T(8,128)(2,1)S(1)}, bf16[2,192,128]{2,1,0:T(8,128)(2,1)S(1)}, u32[]{:S(2)}, u32[]{:S(2)}) collective-permute-start(bf16[2,192,128]{2,1,0:T(8,128)(2,1)S(1)} %select_select_fusion.1), channel_id=1, source_target_pairs={{0,1},{1,0},{2,26},{3,2},{4,20},{5,4},{6,7},{7,6},{8,14},{9,8},{10... | collective-permute-start | bytes 294920 | tf_op jit(solution)/shard_map/ppermute | solution.py:147
  10.5 1.9 %collective-permute-start.5 = (bf16[2,192,128]{2,1,0:T(8,128)(2,1)S(1)}, bf16[2,192,128]{2,1,0:T(8,128)(2,1)S(1)}, u32[]{:S(2)}, u32[]{:S(2)}) collective-permute-start(bf16[2,192,128]{2,1,0:T(8,128)(2,1)S(1)} %select_select_fusion.1), channel_id=1, source_target_pairs={{0,1},{1,0},{2,10},{3,2},{4,6},{5,4},{6,7},{7,3},{8,12},{9,8},{10,... | collective-permute-start | bytes 294920 | tf_op jit(solution)/shard_map/ppermute | solution.py:147
  10.7 5.5 %copy-start = (bf16[192,1024]{1,0:T(8,128)(2,1)S(1)}, bf16[192,1024]{1,0:T(8,128)(2,1)}, u32[]{:S(2)}) copy-start(bf16[192,1024]{1,0:T(8,128)(2,1)} %refs_0_.5) | copy-start | bytes 1179652
  12.4 7.7 %collective-permute-start.7 = (bf16[4,192,128]{2,1,0:T(8,128)(2,1)S(1)}, bf16[4,192,128]{2,1,0:T(8,128)(2,1)S(1)}, u32[]{:S(2)}, u32[]{:S(2)}) collective-permute-start(bf16[4,192,128]{2,1,0:T(8,128)(2,1)S(1)} %pad_maximum_fusion), channel_id=1, source_target_pairs={{0,1},{1,0},{2,3},{3,2},{4,5},{5,4},{6,7},{7,6},{8,9},{9,8},{10,11... | collective-permute-start | bytes 589832 | tf_op jit(solution)/shard_map/ppermute | solution.py:144

commit v2 on v1

--- a/solution.py
+++ b/solution.py
@@ -11,7 +11,7 @@
 HD = 128
 AXIS = "seq"
 FANOUT = 2
-PAIR = 2
+CHUNK = 512
 LOG2E = math.log2(math.e)
 VMEM = pl.BlockSpec(memory_space=pltpu.VMEM)
 
@@ -70,28 +70,48 @@
     return hit
 
 
-def attend_body(blocks, first, last, *refs):
+def chunk_of(rows):
+    return max(c for c in range(HD, rows + 1, HD) if rows % c == 0 and (c <= CHUNK or c == HD))
+
+
+def attend_body(blocks, first, last, carried, *refs):
     it = iter(refs)
     q_ref = next(it)
     kv = [next(it) for _ in range(blocks)]
+    tok = kv[0].shape[1]
     if not first:
         m_in, l_in, a_in = next(it), next(it), next(it)
+    if carried:
+        carry_in = next(it)
     if last:
         o_ref = next(it)
     else:
         m_out, l_out, a_out = next(it), next(it), next(it)
-    tok, width = q_ref.shape
-    heads = width // HD
-    group = math.gcd(heads, PAIR)
+    if carried:
+        carry_out = next(it)
+        carry_out[...] = carry_in[...]
+    stacked = next(it) if first else q_ref
+    rows = stacked.shape[0]
+    chunk = chunk_of(rows)
+    if first:
+        for h in range(rows // tok):
+            stacked[pl.ds(h * tok, tok), :] = q_ref[:, pl.ds(h * HD, HD)]
     keys = [r[0] for r in kv]
     vals = [r[1].T for r in kv]
     keys = keys[0] if blocks == 1 else jnp.concatenate(keys, axis=0)
     vals = vals[0] if blocks == 1 else jnp.concatenate(vals, axis=1)
-    for g in range(0, heads, group):
-        q = jnp.concatenate([q_ref[:, pl.ds(h * HD, HD)] for h in range(g, g + group)], axis=0)
-        cols = pl.ds(g * tok, group * tok)
-        s = lax.dot_general(keys, q, (((1,), (1,)), ((), ())), preferred_element_type=jnp.float32)
-        s = s * (LOG2E / math.sqrt(HD))
+
+    def scores(at):
+        return lax.dot_general(
+            keys, stacked[pl.ds(at, chunk), :], (((1,), (1,)), ((), ())), preferred_element_type=jnp.float32
+        )
+
+    ahead = scores(0)
+    for at in range(0, rows, chunk):
+        s = ahead * (LOG2E / math.sqrt(HD))
+        if at + chunk < rows:
+            ahead = scores(at + chunk)
+        cols = pl.ds(at, chunk)
         top = jnp.max(s, axis=0, keepdims=True)
         if not first:
             old = m_in[:, cols]
@@ -104,31 +124,40 @@
             total = total + alpha * l_in[:, cols]
             out = out + alpha * a_in[:, cols]
         if last:
-            out = (out / total).T.astype(o_ref.dtype)
-            for h in range(group):
-                o_ref[:, pl.ds((g + h) * HD, HD)] = out[h * tok : (h + 1) * tok]
+            out = (out * (1.0 / total)).astype(o_ref.dtype).T
+            done = at
+            while done < at + chunk:
+                h, t = divmod(done, tok)
+                n = min(tok - t, at + chunk - done)
+                o_ref[pl.ds(t, n), pl.ds(h * HD, HD)] = out[done - at : done - at + n]
+                done += n
         else:
             m_out[:, cols] = top
             l_out[:, cols] = total
             a_out[:, cols] = out
 
 
-def attend(queries, blocks, state=None, last=False):
-    tok, width = queries.shape
-    rows = width // HD * tok
+def attend(queries, blocks, state=None, last=False, carry=None):
+    tok = blocks[0].shape[1]
+    rows = queries.size // HD
     if last:
-        out_shape, out_specs = jax.ShapeDtypeStruct((tok, width), queries.dtype), VMEM
+        out_shape = (jax.ShapeDtypeStruct((tok, rows // tok * HD), queries.dtype),)
     else:
         out_shape = tuple(pltpu.VMEM((n, rows), jnp.float32) for n in (1, 1, HD))
-        out_specs = (VMEM,) * 3
     args = [queries, *blocks, *(state or ())]
-    args = [pltpu.with_memory_space_constraint(a, pltpu.VMEM) for a in args]
+    if carry is not None:
+        args.append(carry)
+        out_shape += (pltpu.VMEM(carry.shape, carry.dtype),)
+    if state is None:
+        out_shape += (pltpu.VMEM((rows, HD), queries.dtype),)
+    else:
+        args = [pltpu.with_memory_space_constraint(a, pltpu.VMEM) for a in args]
     pairs = rows * sum(b.shape[1] for b in blocks)
     return pl.pallas_call(
-        functools.partial(attend_body, len(blocks), state is None, last),
+        functools.partial(attend_body, len(blocks), state is None, last, carry is not None),
         out_shape=out_shape,
         in_specs=[VMEM] * len(args),
-        out_specs=out_specs,
+        out_specs=(VMEM,) * len(out_shape),
         compiler_params=pltpu.CompilerParams(vmem_limit_bytes=24 << 20),
         cost_estimate=pl.CostEstimate(flops=4 * pairs * HD, bytes_accessed=0, transcendentals=pairs),
     )(*args)
@@ -147,26 +176,28 @@
         return lax.ppermute(value, AXIS, fill(real, count))
 
     received = {}
-    first = None
+    *state, own, queries = attend(queries, [keyval], carry=keyval)
+    first = own
     informed = [0, 1]
-    for bit in [*range(levels - 1, max(levels - 3, 0), -1), None, *range(max(levels - 3, 0), 0, -1)]:
+    for bit in [*range(1, levels - 1), None, levels - 1]:
         if bit is None:
             got, holder = send(keyval, [(0, far)]), far
         else:
             got, holder = swap(keyval, bit), 1 << bit
             received[bit] = got
         informed.append(holder)
-        first = got if first is None else jnp.where(me == holder, got, first)
-    state = attend(queries, [keyval])
-    for wave in plan(informed, count):
+        first = jnp.where(me == holder, got, first)
+    received[0] = swap(own, 0)
+    arrived = [received[bit] for bit in reversed(range(levels))]
+    waves = plan(informed, count)
+    for k, wave in enumerate(waves):
         came = [(send(first, real), [t for _, t in real]) for real in wave]
+        if k + 1 == len(waves):
+            *state, first = attend(queries, arrived, state, carry=first)
         for got, holders in came:
             first = jnp.where(member(me, holders), got, first)
-    state = attend(queries, [received[bit] for bit in range(1, levels)], state)
-    first = jnp.where(me == 0, keyval, first)
-    both = swap(jnp.concatenate([keyval, first], axis=0), 0)
-    first = jnp.where(me % 2 == 1, both[2:], first)
-    return attend(queries, [both[:2], first], state, last=True)
+    first = jnp.where(me % 2 == 1, swap(first, 0), first)
+    return attend(queries, [first], state, last=True)[0]
 
 
 def solution(mesh):

time: 22.8 us -> 19.5 us (0.86)
  the two profiles are of different devices: /device:TPU:11 before, /device:TPU:9 now
where the time goes in v2:
time: 19.5 us; the launch traced here: 19.3 us
  starting transfers between devices  7.96 us (41%)
  Pallas kernels  4.89 us (25%)
  waiting for transfers between devices  4.44 us (23%)
  local copies, waits for them, and re-layouts  1.89 us (10%)
    ppermute x6, starting transfers between devices, swap(): return lax.ppermute(value, AXIS, [(i, i ^ 1 << bit) for i in range(count)])  5.1 us
    pallas_call x3, Pallas kernels, attend(): pl.pallas_call(functools.partial(attend_body, len(blocks), state is None,...  4.89 us
    ppermute x3, waiting for transfers between devices, send(): return lax.ppermute(value, AXIS, fill(real, count))  3.02 us
    ppermute x3, starting transfers between devices, send(): return lax.ppermute(value, AXIS, fill(real, count))  2.87 us
    unnamed x4, local copies, waits for them, and re-layouts  1.89 us
    ppermute x6, waiting for transfers between devices, swap(): return lax.ppermute(value, AXIS, [(i, i ^ 1 << bit) for i in range(count)])  1.42 us
  transfers between devices with their start and end apart: 9, of which 3 were waited for; matrix products, arithmetic and copies ran while one was open for 0% of the time, Pallas kernels for 17%

profile of v2, /device:TPU:9, one launch (start us, length us, event | category | flops | bytes accessed | tf_op | source)
XLA Modules:
  0.0 19.3 jit_solution(5887254520803242549)
XLA Ops:
  0.0 2.3 %collective-permute-start = (bf16[2,192,128]{2,1,0:T(8,128)(2,1)}, bf16[2,192,128]{2,1,0:T(8,128)(2,1)S(1)}, u32[]{:S(2)}, u32[]{:S(2)}) collective-permute-start(bf16[2,192,128]{2,1,0:T(8,128)(2,1)} %refs_2_.1), channel_id=1, source_target_pairs={{0,16},{1,17},{2,18},{3,19},{4,20},{5,21},{6,22},{7,23},{8,24},{9,... | collective-permute-start | bytes 294920 | tf_op jit(solution)/shard_map/ppermute | solution.py:173
  2.3 0.2 collective-permute-start.2
  2.5 1.2 %collective-permute-start.3 = (bf16[2,192,128]{2,1,0:T(8,128)(2,1)}, bf16[2,192,128]{2,1,0:T(8,128)(2,1)S(1)}, u32[]{:S(2)}, u32[]{:S(2)}) collective-permute-start(bf16[2,192,128]{2,1,0:T(8,128)(2,1)} %refs_2_.1), channel_id=1, source_target_pairs={{0,4},{1,5},{2,6},{3,7},{4,0},{5,1},{6,2},{7,3},{8,12},{9,13},{10,... | collective-permute-start | bytes 294920 | tf_op jit(solution)/shard_map/ppermute | solution.py:173
  3.7 1.2 %collective-permute-start.4 = (bf16[2,192,128]{2,1,0:T(8,128)(2,1)}, bf16[2,192,128]{2,1,0:T(8,128)(2,1)S(1)}, u32[]{:S(2)}, u32[]{:S(2)}) collective-permute-start(bf16[2,192,128]{2,1,0:T(8,128)(2,1)} %refs_2_.1), channel_id=1, source_target_pairs={{0,2},{1,3},{2,0},{3,1},{4,6},{5,7},{6,4},{7,5},{8,10},{9,11},{10,... | collective-permute-start | bytes 294920 | tf_op jit(solution)/shard_map/ppermute | solution.py:173
  4.9 1.8 %collective-permute-start.1 = (bf16[2,192,128]{2,1,0:T(8,128)(2,1)}, bf16[2,192,128]{2,1,0:T(8,128)(2,1)S(1)}, u32[]{:S(2)}, u32[]{:S(2)}) collective-permute-start(bf16[2,192,128]{2,1,0:T(8,128)(2,1)} %refs_2_.1), channel_id=1, source_target_pairs={{0,24},{1,0},{2,3},{3,2},{4,5},{5,4},{6,7},{7,6},{8,9},{9,8},{10,1... | collective-permute-start | bytes 294920 | tf_op jit(solution)/shard_map/ppermute | solution.py:176
  6.7 0.0 copy-start
  6.7 0.9 %copy-done = bf16[2,192,128]{2,1,0:T(8,128)(2,1)S(1)} copy-done((bf16[2,192,128]{2,1,0:T(8,128)(2,1)S(1)}, bf16[2,192,128]{2,1,0:T(8,128)(2,1)}, u32[]{:S(2)}) %copy-start) | copy-done | bytes 98328
  7.6 0.0 copy-start.1
  7.6 1.0 %copy-done.1 = bf16[192,1024]{1,0:T(8,128)(2,1)S(1)} copy-done((bf16[192,1024]{1,0:T(8,128)(2,1)S(1)}, bf16[192,1024]{1,0:T(8,128)(2,1)}, u32[]{:S(2)}) %copy-start.1) | copy-done | bytes 393240
  8.6 0.8 %shard_map.28 = (f32[1,1536]{1,0:T(1,128)S(1)}, f32[1,1536]{1,0:T(1,128)S(1)}, f32[128,1536]{1,0:T(8,128)S(1)}, bf16[2,192,128]{2,1,0:T(8,128)(2,1)S(1)}, bf16[1536,128]{1,0:T(8,128)(2,1)S(1)}) custom-call(bf16[192,1024]{1,0:T(8,128)(2,1)S(1)} %copy-done.1, bf16[2,192,128]{2,1,0:T(8,128)(2,1)S(1)} %copy-done, bf16[2,192,128]{2,1,0:T(8,128)(2,1)S(1)} %copy-done), custom_call_target="tpu_custom_call" | custom-call | flops 150994944 | tf_op jit(solution)/shard_map/pallas_call | solution.py:156
  9.4 0.0 collective-permute-done.refs_1_
  9.4 0.1 collective-permute-start.7
  9.5 0.0 collective-permute-done.2.refs_2_
  9.5 0.0 collective-permute-done.3.refs_3_
  9.5 0.0 collective-permute-done.4.refs_4_
  9.5 0.0 collective-permute-done.1
  9.6 0.6 %collective-permute-start.5 = (bf16[2,192,128]{2,1,0:T(8,128)(2,1)S(1)}, bf16[2,192,128]{2,1,0:T(8,128)(2,1)S(1)}, u32[]{:S(2)}, u32[]{:S(2)}) collective-permute-start(bf16[2,192,128]{2,1,0:T(8,128)(2,1)S(1)} %select_select_fusion.1.refs_9_), channel_id=1, source_target_pairs={{0,1},{1,0},{2,10},{3,2},{4,6},{5,4},{6,7},{7,3},{8,12},{9,8},{10,... | collective-permute-start | bytes 294920 | tf_op jit(solution)/shard_map/ppermute | solution.py:176
  10.2 0.5 %collective-permute-start.6 = (bf16[2,192,128]{2,1,0:T(8,128)(2,1)S(1)}, bf16[2,192,128]{2,1,0:T(8,128)(2,1)S(1)}, u32[]{:S(2)}, u32[]{:S(2)}) collective-permute-start(bf16[2,192,128]{2,1,0:T(8,128)(2,1)S(1)} %select_select_fusion.1.refs_9_), channel_id=1, source_target_pairs={{0,1},{1,0},{2,26},{3,2},{4,20},{5,4},{6,7},{7,6},{8,14},{9,8},{10... | collective-permute-start | bytes 294920 | tf_op jit(solution)/shard_map/ppermute | solution.py:176
  10.7 0.1 collective-permute-done.7.refs_5_
  10.8 2.5 %shard_map.29 = (f32[1,1536]{1,0:T(1,128)S(1)}, f32[1,1536]{1,0:T(1,128)S(1)}, f32[128,1536]{1,0:T(8,128)S(1)}, bf16[2,192,128]{2,1,0:T(8,128)(2,1)S(1)}) custom-call(bf16[1536,128]{1,0:T(8,128)(2,1)S(1)} %get-tuple-element.14.refs_0_, bf16[2,192,128]{2,1,0:T(8,128)(2,1)S(1)} %collective-permute-done.refs_1_, ...), custom_call_target="tpu_custom_call" | custom-call | flops 754974720 | tf_op jit(solution)/shard_map/pallas_call | solution.py:156
  13.3 0.0 collective-permute-done.5
  13.3 3.0 %collective-permute-done.6 = bf16[2,192,128]{2,1,0:T(8,128)(2,1)S(1)} collective-permute-done((bf16[2,192,128]{2,1,0:T(8,128)(2,1)S(1)}, bf16[2,192,128]{2,1,0:T(8,128)(2,1)S(1)}, u32[]{:S(2)}, u32[]{:S(2)}) %collective-permute-start.6) | collective-permute-done | bytes 98336 | tf_op jit(solution)/shard_map/ppermute | solution.py:176
  16.3 0.1 collective-permute-start.8
  16.4 1.3 %collective-permute-done.8 = bf16[2,192,128]{2,1,0:T(8,128)(2,1)S(1)} collective-permute-done((bf16[2,192,128]{2,1,0:T(8,128)(2,1)S(1)}, bf16[2,192,128]{2,1,0:T(8,128)(2,1)S(1)}, u32[]{:S(2)}, u32[]{:S(2)}) %collective-permute-start.8) | collective-permute-done | bytes 98336 | tf_op jit(solution)/shard_map/ppermute | solution.py:173
  17.7 1.6 %shard_map.30 = bf16[192,1024]{1,0:T(8,128)(2,1)} custom-call(bf16[1536,128]{1,0:T(8,128)(2,1)S(1)} %get-tuple-element.14.refs_0_, bf16[2,192,128]{2,1,0:T(8,128)(2,1)S(1)} %broadcast_select_fusion.refs_1_, f32[1,1536]{1,0:T(1,128)S(1)} %get-tuple-element.20.refs_2_, f32[1,1536]{1,0:T(1,128)S(1)} %get-tuple-element.21.refs_3_, ...), custom_call_target="tpu_custom_call" | custom-call | flops 150994944 | tf_op jit(solution)/shard_map/pallas_call | solution.py:156
  (3 shorter events, 0.1 us)
Async XLA Ops:
  0.0 9.4 %collective-permute-start = (bf16[2,192,128]{2,1,0:T(8,128)(2,1)}, bf16[2,192,128]{2,1,0:T(8,128)(2,1)S(1)}, u32[]{:S(2)}, u32[]{:S(2)}) collective-permute-start(bf16[2,192,128]{2,1,0:T(8,128)(2,1)} %refs_2_.1), channel_id=1, source_target_pairs={{0,16},{1,17},{2,18},{3,19},{4,20},{5,21},{6,22},{7,23},{8,24},{9,... | collective-permute-start | bytes 294920 | tf_op jit(solution)/shard_map/ppermute | solution.py:173
  2.3 7.2 %collective-permute-start.2 = (bf16[2,192,128]{2,1,0:T(8,128)(2,1)}, bf16[2,192,128]{2,1,0:T(8,128)(2,1)S(1)}, u32[]{:S(2)}, u32[]{:S(2)}) collective-permute-start(bf16[2,192,128]{2,1,0:T(8,128)(2,1)} %refs_2_.1), channel_id=1, source_target_pairs={{0,8},{1,9},{2,10},{3,11},{4,12},{5,13},{6,14},{7,15},{8,0},{9,1},... | collective-permute-start | bytes 294920 | tf_op jit(solution)/shard_map/ppermute | solution.py:173
  2.5 7.1 %collective-permute-start.3 = (bf16[2,192,128]{2,1,0:T(8,128)(2,1)}, bf16[2,192,128]{2,1,0:T(8,128)(2,1)S(1)}, u32[]{:S(2)}, u32[]{:S(2)}) collective-permute-start(bf16[2,192,128]{2,1,0:T(8,128)(2,1)} %refs_2_.1), channel_id=1, source_target_pairs={{0,4},{1,5},{2,6},{3,7},{4,0},{5,1},{6,2},{7,3},{8,12},{9,13},{10,... | collective-permute-start | bytes 294920 | tf_op jit(solution)/shard_map/ppermute | solution.py:173
  3.7 5.8 %collective-permute-start.4 = (bf16[2,192,128]{2,1,0:T(8,128)(2,1)}, bf16[2,192,128]{2,1,0:T(8,128)(2,1)S(1)}, u32[]{:S(2)}, u32[]{:S(2)}) collective-permute-start(bf16[2,192,128]{2,1,0:T(8,128)(2,1)} %refs_2_.1), channel_id=1, source_target_pairs={{0,2},{1,3},{2,0},{3,1},{4,6},{5,7},{6,4},{7,5},{8,10},{9,11},{10,... | collective-permute-start | bytes 294920 | tf_op jit(solution)/shard_map/ppermute | solution.py:173
  4.9 4.6 %collective-permute-start.1 = (bf16[2,192,128]{2,1,0:T(8,128)(2,1)}, bf16[2,192,128]{2,1,0:T(8,128)(2,1)S(1)}, u32[]{:S(2)}, u32[]{:S(2)}) collective-permute-start(bf16[2,192,128]{2,1,0:T(8,128)(2,1)} %refs_2_.1), channel_id=1, source_target_pairs={{0,24},{1,0},{2,3},{3,2},{4,5},{5,4},{6,7},{7,6},{8,9},{9,8},{10,1... | collective-permute-start | bytes 294920 | tf_op jit(solution)/shard_map/ppermute | solution.py:176
  6.7 0.9 %copy-start = (bf16[2,192,128]{2,1,0:T(8,128)(2,1)S(1)}, bf16[2,192,128]{2,1,0:T(8,128)(2,1)}, u32[]{:S(2)}) copy-start(bf16[2,192,128]{2,1,0:T(8,128)(2,1)} %refs_2_.1) | copy-start | bytes 294916
  7.6 1.0 %copy-start.1 = (bf16[192,1024]{1,0:T(8,128)(2,1)S(1)}, bf16[192,1024]{1,0:T(8,128)(2,1)}, u32[]{:S(2)}) copy-start(bf16[192,1024]{1,0:T(8,128)(2,1)} %refs_0_.1) | copy-start | bytes 1179652
  9.4 1.4 %collective-permute-start.7 = (bf16[2,192,128]{2,1,0:T(8,128)(2,1)S(1)}, bf16[2,192,128]{2,1,0:T(8,128)(2,1)S(1)}, u32[]{:S(2)}, u32[]{:S(2)}) collective-permute-start(bf16[2,192,128]{2,1,0:T(8,128)(2,1)S(1)} %get-tuple-element.15), channel_id=1, source_target_pairs={{0,1},{1,0},{2,3},{3,2},{4,5},{5,4},{6,7},{7,6},{8,9},{9,8},{10,11... | collective-permute-start | bytes 294920 | tf_op jit(solution)/shard_map/ppermute | solution.py:173
  9.6 3.7 %collective-permute-start.5 = (bf16[2,192,128]{2,1,0:T(8,128)(2,1)S(1)}, bf16[2,192,128]{2,1,0:T(8,128)(2,1)S(1)}, u32[]{:S(2)}, u32[]{:S(2)}) collective-permute-start(bf16[2,192,128]{2,1,0:T(8,128)(2,1)S(1)} %select_select_fusion.1.refs_9_), channel_id=1, source_target_pairs={{0,1},{1,0},{2,10},{3,2},{4,6},{5,4},{6,7},{7,3},{8,12},{9,8},{10,... | collective-permute-start | bytes 294920 | tf_op jit(solution)/shard_map/ppermute | solution.py:176
  10.2 6.2 %collective-permute-start.6 = (bf16[2,192,128]{2,1,0:T(8,128)(2,1)S(1)}, bf16[2,192,128]{2,1,0:T(8,128)(2,1)S(1)}, u32[]{:S(2)}, u32[]{:S(2)}) collective-permute-start(bf16[2,192,128]{2,1,0:T(8,128)(2,1)S(1)} %select_select_fusion.1.refs_9_), channel_id=1, source_target_pairs={{0,1},{1,0},{2,26},{3,2},{4,20},{5,4},{6,7},{7,6},{8,14},{9,8},{10... | collective-permute-start | bytes 294920 | tf_op jit(solution)/shard_map/ppermute | solution.py:176
  16.3 1.4 %collective-permute-start.8 = (bf16[2,192,128]{2,1,0:T(8,128)(2,1)S(1)}, bf16[2,192,128]{2,1,0:T(8,128)(2,1)S(1)}, u32[]{:S(2)}, u32[]{:S(2)}) collective-permute-start(bf16[2,192,128]{2,1,0:T(8,128)(2,1)S(1)} %select_select_fusion), channel_id=1, source_target_pairs={{0,1},{1,0},{2,3},{3,2},{4,5},{5,4},{6,7},{7,6},{8,9},{9,8},{10,11... | collective-permute-start | bytes 294920 | tf_op jit(solution)/shard_map/ppermute | solution.py:173

commit v3 on v2

--- a/solution.py
+++ b/solution.py
@@ -10,10 +10,12 @@
 
 HD = 128
 AXIS = "seq"
-FANOUT = 2
+FANOUT = 3
 CHUNK = 512
+LAST_CHUNK = 768
 LOG2E = math.log2(math.e)
 VMEM = pl.BlockSpec(memory_space=pltpu.VMEM)
+TINY = pl.CostEstimate(flops=1, bytes_accessed=1, transcendentals=0)
 
 
 def hops(a, b):
@@ -41,25 +43,23 @@
     return sorted(goes.items())
 
 
-def plan(informed, count):
-    informed = set(informed)
-    missing = [t for t in range(0, count, 2) if t not in informed]
+def plan(seeds, later, count):
+    slots = {s: list(range(FANOUT)) for s in seeds} | {s: [FANOUT - 1] for s in later}
+    holders = {0, *slots} | {1 << b for b in range(count.bit_length() - 1)}
+    missing = [t for t in range(0, count, 2) if t not in holders]
     waves = []
     while missing:
-        sends = {s: [] for s in sorted(informed) if s}
-        order = sorted(missing, key=lambda t: (-min(hops(s, t) for s in sends), -t))
-        for t in order:
-            free = [s for s in sends if len(sends[s]) < FANOUT]
+        wave = [[] for _ in range(FANOUT)]
+        for t in sorted(missing, key=lambda t: (-min(hops(s, t) for s in slots), -t)):
+            free = [s for s in slots if slots[s]]
             if not free:
                 break
-            s = min(free, key=lambda s: (hops(s, t), len(sends[s]), -s))
-            sends[s].append(t)
-        wave = [[(s, ts[k]) for s, ts in sends.items() if len(ts) > k] for k in range(FANOUT)]
-        wave = [w for w in wave if w]
-        waves.append(wave)
-        reached = {t for w in wave for _, t in w}
-        informed |= reached
-        missing = [t for t in missing if t not in reached]
+            s = min(free, key=lambda s: (hops(s, t), -s))
+            wave[slots[s].pop(0)].append((s, t))
+        waves.append([w for w in wave if w])
+        holders |= {t for w in wave for _, t in w}
+        slots = {s: list(range(FANOUT)) for s in holders}
+        missing = [t for t in missing if t not in holders]
     return waves
 
 
@@ -70,8 +70,8 @@
     return hit
 
 
-def chunk_of(rows):
-    return max(c for c in range(HD, rows + 1, HD) if rows % c == 0 and (c <= CHUNK or c == HD))
+def chunk_of(rows, limit):
+    return max(c for c in range(HD, rows + 1, HD) if rows % c == 0 and (c <= limit or c == HD))
 
 
 def attend_body(blocks, first, last, carried, *refs):
@@ -92,7 +92,7 @@
         carry_out[...] = carry_in[...]
     stacked = next(it) if first else q_ref
     rows = stacked.shape[0]
-    chunk = chunk_of(rows)
+    chunk = chunk_of(rows, LAST_CHUNK if last else CHUNK)
     if first:
         for h in range(rows // tok):
             stacked[pl.ds(h * tok, tok), :] = q_ref[:, pl.ds(h * HD, HD)]
@@ -150,8 +150,7 @@
         out_shape += (pltpu.VMEM(carry.shape, carry.dtype),)
     if state is None:
         out_shape += (pltpu.VMEM((rows, HD), queries.dtype),)
-    else:
-        args = [pltpu.with_memory_space_constraint(a, pltpu.VMEM) for a in args]
+    args = [pltpu.with_memory_space_constraint(a, pltpu.VMEM) for a in args]
     pairs = rows * sum(b.shape[1] for b in blocks)
     return pl.pallas_call(
         functools.partial(attend_body, len(blocks), state is None, last, carry is not None),
@@ -163,11 +162,47 @@
     )(*args)
 
 
+def hold_body(block_ref, after_ref, out_ref):
+    out_ref[...] = block_ref[...]
+
+
+def hold(block, after):
+    args = [pltpu.with_memory_space_constraint(a, pltpu.VMEM) for a in (block, after)]
+    return pl.pallas_call(
+        hold_body,
+        out_shape=pltpu.VMEM(block.shape, block.dtype),
+        in_specs=[VMEM, pl.BlockSpec(memory_space=pl.ANY)],
+        out_specs=VMEM,
+        cost_estimate=TINY,
+    )(*args)
+
+
+def pick_body(holders, *refs):
+    *blocks, out_ref = refs
+    me = lax.axis_index(AXIS)
+    for block, holder in zip(blocks, holders):
+
+        @pl.when(me == holder)
+        def _():
+            out_ref[...] = block[...]
+
+
+def pick(blocks):
+    args = [pltpu.with_memory_space_constraint(b, pltpu.VMEM) for b in blocks.values()]
+    return pl.pallas_call(
+        functools.partial(pick_body, tuple(blocks)),
+        out_shape=pltpu.VMEM(args[0].shape, args[0].dtype),
+        in_specs=[VMEM] * len(args),
+        out_specs=VMEM,
+        cost_estimate=TINY,
+    )(*args)
+
+
 def on_device(queries, keyval):
     count = lax.axis_size(AXIS)
     levels = count.bit_length() - 1
     me = lax.axis_index(AXIS)
-    far = 3 << levels - 2
+    high, top = 1 << levels - 2, 1 << levels - 1
 
     def swap(value, bit):
         return lax.ppermute(value, AXIS, [(i, i ^ 1 << bit) for i in range(count)])
@@ -175,29 +210,35 @@
     def send(value, real):
         return lax.ppermute(value, AXIS, fill(real, count))
 
-    received = {}
-    *state, own, queries = attend(queries, [keyval], carry=keyval)
-    first = own
-    informed = [0, 1]
-    for bit in [*range(1, levels - 1), None, levels - 1]:
-        if bit is None:
-            got, holder = send(keyval, [(0, far)]), far
-        else:
-            got, holder = swap(keyval, bit), 1 << bit
-            received[bit] = got
-        informed.append(holder)
-        first = jnp.where(me == holder, got, first)
-    received[0] = swap(own, 0)
-    arrived = [received[bit] for bit in reversed(range(levels))]
-    waves = plan(informed, count)
+    received = {bit: swap(keyval, bit) for bit in range(1, levels)}
+    seeds = {high: received[levels - 2]}
+    seeds |= {holder: send(keyval, [(0, holder)]) for holder in (high | top, top)}
+    first = pick(seeds)
+    own = hold(keyval, first)
+    later = {4: received[2]}
+    waves = plan(list(seeds), list(later), count)
     for k, wave in enumerate(waves):
-        came = [(send(first, real), [t for _, t in real]) for real in wave]
+        came = []
+        for real in wave:
+            if k == 0 and real is wave[-1]:
+                for holder, got in (later | {0: own}).items():
+                    first = jnp.where(me == holder, got, first)
+            came.append((send(first, real), [t for _, t in real]))
+        if k == 0:
+            for bit in range(1, levels - 2):
+                if 1 << bit not in later:
+                    first = jnp.where(me == 1 << bit, received[bit], first)
+            received[0] = jnp.where(me == top, seeds[high | top], seeds[top])
+            received[0] = jnp.where(me == 1, came[-1][0], received[0])
         if k + 1 == len(waves):
-            *state, first = attend(queries, arrived, state, carry=first)
+            *state, stacked = attend(queries, [own, *(received[bit] for bit in range(levels - 2, 0, -1))])
+            *state, first = attend(stacked, [received[levels - 1]], state, carry=first)
         for got, holders in came:
             first = jnp.where(member(me, holders), got, first)
-    first = jnp.where(me % 2 == 1, swap(first, 0), first)
-    return attend(queries, [first], state, last=True)[0]
+    passed = swap(first, 0)
+    state = attend(stacked, [received[0]], state)
+    first = jnp.where(me % 2 == 1, passed, first)
+    return attend(stacked, [first], state, last=True)[0]
 
 
 def solution(mesh):

time: 19.5 us -> 18.1 us (0.928)
  the two profiles are of different devices: /device:TPU:9 before, /device:TPU:17 now
where the time goes in v3:
time: 18.1 us; the launch traced here: 18 us
  starting transfers between devices  8.26 us (46%)
  Pallas kernels  4.84 us (27%)
  waiting for transfers between devices  4.17 us (23%)
  local copies, waits for them, and re-layouts  0.54 us (3%)
    pallas_call x4, Pallas kernels, attend(): pl.pallas_call(functools.partial(attend_body, len(blocks), state is None,...  4.83 us
    ppermute x5, starting transfers between devices, send(): return lax.ppermute(value, AXIS, fill(real, count))  4.34 us
    ppermute x5, starting transfers between devices, swap(): return lax.ppermute(value, AXIS, [(i, i ^ 1 << bit) for i in range(count)])  3.92 us
    ppermute x5, waiting for transfers between devices, swap(): return lax.ppermute(value, AXIS, [(i, i ^ 1 << bit) for i in range(count)])  2.16 us
    ppermute x5, waiting for transfers between devices, send(): return lax.ppermute(value, AXIS, fill(real, count))  2.01 us
    unnamed x4, local copies, waits for them, and re-layouts  0.54 us
  transfers between devices with their start and end apart: 10, of which 5 were waited for; matrix products, arithmetic and copies ran while one was open for 0% of the time, Pallas kernels for 19%

profile of v3, /device:TPU:17, one launch (start us, length us, event | category | flops | bytes accessed | tf_op | source)
XLA Modules:
  0.0 18.0 jit_solution(11943257300056440332)
XLA Ops:
  0.0 1.3 %collective-permute-start = (bf16[2,192,128]{2,1,0:T(8,128)(2,1)}, bf16[2,192,128]{2,1,0:T(8,128)(2,1)S(1)}, u32[]{:S(2)}, u32[]{:S(2)}) collective-permute-start(bf16[2,192,128]{2,1,0:T(8,128)(2,1)} %block_ref.1), channel_id=1, source_target_pairs={{0,8},{1,9},{2,10},{3,11},{4,12},{5,13},{6,14},{7,15},{8,0},{9,1},... | collective-permute-start | bytes 294920 | tf_op jit(solution)/shard_map/ppermute | solution.py:208
  1.3 1.0 %collective-permute-start.1 = (bf16[2,192,128]{2,1,0:T(8,128)(2,1)}, bf16[2,192,128]{2,1,0:T(8,128)(2,1)S(1)}, u32[]{:S(2)}, u32[]{:S(2)}) collective-permute-start(bf16[2,192,128]{2,1,0:T(8,128)(2,1)} %block_ref.1), channel_id=1, source_target_pairs={{0,24},{1,0},{2,3},{3,2},{4,5},{5,4},{6,7},{7,6},{8,9},{9,8},{10,1... | collective-permute-start | bytes 294920 | tf_op jit(solution)/shard_map/ppermute | solution.py:211
  2.3 0.1 collective-permute-start.2
  2.3 1.2 %collective-permute-start.3 = (bf16[2,192,128]{2,1,0:T(8,128)(2,1)}, bf16[2,192,128]{2,1,0:T(8,128)(2,1)S(1)}, u32[]{:S(2)}, u32[]{:S(2)}) collective-permute-start(bf16[2,192,128]{2,1,0:T(8,128)(2,1)} %block_ref.1), channel_id=1, source_target_pairs={{0,4},{1,5},{2,6},{3,7},{4,0},{5,1},{6,2},{7,3},{8,12},{9,13},{10,... | collective-permute-start | bytes 294920 | tf_op jit(solution)/shard_map/ppermute | solution.py:208
  3.5 1.2 %collective-permute-start.4 = (bf16[2,192,128]{2,1,0:T(8,128)(2,1)}, bf16[2,192,128]{2,1,0:T(8,128)(2,1)S(1)}, u32[]{:S(2)}, u32[]{:S(2)}) collective-permute-start(bf16[2,192,128]{2,1,0:T(8,128)(2,1)} %block_ref.1), channel_id=1, source_target_pairs={{0,2},{1,3},{2,0},{3,1},{4,6},{5,7},{6,4},{7,5},{8,10},{9,11},{10,... | collective-permute-start | bytes 294920 | tf_op jit(solution)/shard_map/ppermute | solution.py:208
  4.7 0.0 copy-start
  4.7 0.0 collective-permute-done.refs_0_.refs_2_
  4.7 0.2 collective-permute-start.8
  4.9 0.0 collective-permute-done.1.refs_1_
  4.9 0.2 %collective-permute-done.2.refs_2_ = bf16[2,192,128]{2,1,0:T(8,128)(2,1)S(1)} collective-permute-done((bf16[2,192,128]{2,1,0:T(8,128)(2,1)}, bf16[2,192,128]{2,1,0:T(8,128)(2,1)S(1)}, u32[]{:S(2)}, u32[]{:S(2)}) %collective-permute-start.2) | collective-permute-done | bytes 98336 | tf_op jit(solution)/shard_map/ppermute | solution.py:211
  5.1 0.5 %copy-done = bf16[2,192,128]{2,1,0:T(8,128)(2,1)S(1)} copy-done((bf16[2,192,128]{2,1,0:T(8,128)(2,1)S(1)}, bf16[2,192,128]{2,1,0:T(8,128)(2,1)}, u32[]{:S(2)}) %copy-start) | copy-done | bytes 98328
  5.6 0.0 copy-start.1
  5.6 0.8 %collective-permute-done.3.refs_3_ = bf16[2,192,128]{2,1,0:T(8,128)(2,1)S(1)} collective-permute-done((bf16[2,192,128]{2,1,0:T(8,128)(2,1)}, bf16[2,192,128]{2,1,0:T(8,128)(2,1)S(1)}, u32[]{:S(2)}, u32[]{:S(2)}) %collective-permute-start.3) | collective-permute-done | bytes 98336 | tf_op jit(solution)/shard_map/ppermute | solution.py:208
  6.4 0.9 %collective-permute-done.4.refs_4_ = bf16[2,192,128]{2,1,0:T(8,128)(2,1)S(1)} collective-permute-done((bf16[2,192,128]{2,1,0:T(8,128)(2,1)}, bf16[2,192,128]{2,1,0:T(8,128)(2,1)S(1)}, u32[]{:S(2)}, u32[]{:S(2)}) %collective-permute-start.4) | collective-permute-done | bytes 98336 | tf_op jit(solution)/shard_map/ppermute | solution.py:208
  7.4 1.8 %collective-permute-start.5 = (bf16[2,192,128]{2,1,0:T(8,128)(2,1)S(1)}, bf16[2,192,128]{2,1,0:T(8,128)(2,1)S(1)}, u32[]{:S(2)}, u32[]{:S(2)}) collective-permute-start(bf16[2,192,128]{2,1,0:T(8,128)(2,1)S(1)} %get-tuple-element.28), channel_id=1, source_target_pairs={{0,1},{1,0},{2,3},{3,2},{4,6},{5,4},{6,7},{7,5},{8,10},{9,8},{10,1... | collective-permute-start | bytes 294920 | tf_op jit(solution)/shard_map/ppermute | solution.py:211
  9.2 1.5 %collective-permute-start.6 = (bf16[2,192,128]{2,1,0:T(8,128)(2,1)S(1)}, bf16[2,192,128]{2,1,0:T(8,128)(2,1)S(1)}, u32[]{:S(2)}, u32[]{:S(2)}) collective-permute-start(bf16[2,192,128]{2,1,0:T(8,128)(2,1)S(1)} %shard_map.28.after_ref), channel_id=1, source_target_pairs={{0,1},{1,0},{2,3},{3,2},{4,5},{5,4},{6,7},{7,6},{8,12},{9,8},{10,1... | collective-permute-start | bytes 294920 | tf_op jit(solution)/shard_map/ppermute | solution.py:211
  10.7 0.0 collective-permute-start.7
  10.7 0.0 copy-done.1
  10.7 1.7 %shard_map.30 = (f32[1,1536]{1,0:T(1,128)S(1)}, f32[1,1536]{1,0:T(1,128)S(1)}, f32[128,1536]{1,0:T(8,128)S(1)}, bf16[1536,128]{1,0:T(8,128)(2,1)S(1)}) custom-call(bf16[192,1024]{1,0:T(8,128)(2,1)S(1)} %copy-done.1, bf16[2,192,128]{2,1,0:T(8,128)(2,1)S(1)} %shard_map.29.refs_1_, bf16[2,192,128]{2,1,0:T(8,128)(2,1)S(1)} %collective-permute-done.refs_0_.refs_2_, ...), custom_call_target="tpu_custom_call" | custom-call | flops 603979776 | tf_op jit(solution)/shard_map/pallas_call | solution.py:155
  12.4 0.0 collective-permute-done.8.refs_1_
  12.4 0.8 %shard_map.31 = (f32[1,1536]{1,0:T(1,128)S(1)}, f32[1,1536]{1,0:T(1,128)S(1)}, f32[128,1536]{1,0:T(8,128)S(1)}, bf16[2,192,128]{2,1,0:T(8,128)(2,1)S(1)}) custom-call(bf16[1536,128]{1,0:T(8,128)(2,1)S(1)} %get-tuple-element.16.refs_0_, bf16[2,192,128]{2,1,0:T(8,128)(2,1)S(1)} %collective-permute-done.8.refs_1_, f32[1,1536]{1,0:T(1,128)S(1)} %get-tuple-element.17.refs_2_, ...), custom_call_target="tpu_custom_call" | custom-call | flops 150994944 | tf_op jit(solution)/shard_map/pallas_call | solution.py:155
  13.3 0.0 collective-permute-done.5
  13.3 0.0 collective-permute-done.6
  13.3 1.8 %collective-permute-done.7 = bf16[2,192,128]{2,1,0:T(8,128)(2,1)S(1)} collective-permute-done((bf16[2,192,128]{2,1,0:T(8,128)(2,1)S(1)}, bf16[2,192,128]{2,1,0:T(8,128)(2,1)S(1)}, u32[]{:S(2)}, u32[]{:S(2)}) %collective-permute-start.7) | collective-permute-done | bytes 98336 | tf_op jit(solution)/shard_map/ppermute | solution.py:211
  15.1 0.1 collective-permute-start.9
  15.2 0.8 %shard_map.32 = (f32[1,1536]{1,0:T(1,128)S(1)}, f32[1,1536]{1,0:T(1,128)S(1)}, f32[128,1536]{1,0:T(8,128)S(1)}) custom-call(bf16[1536,128]{1,0:T(8,128)(2,1)S(1)} %get-tuple-element.16.refs_0_, bf16[2,192,128]{2,1,0:T(8,128)(2,1)S(1)} %get-tuple-element.29.refs_1_, f32[1,1536]{1,0:T(1,128)S(1)} %get-tuple-element.21.refs_2_, ...), custom_call_target="tpu_custom_call" | custom-call | flops 150994944 | tf_op jit(solution)/shard_map/pallas_call | solution.py:155
  16.0 0.5 %collective-permute-done.9 = bf16[2,192,128]{2,1,0:T(8,128)(2,1)S(1)} collective-permute-done((bf16[2,192,128]{2,1,0:T(8,128)(2,1)S(1)}, bf16[2,192,128]{2,1,0:T(8,128)(2,1)S(1)}, u32[]{:S(2)}, u32[]{:S(2)}) %collective-permute-start.9) | collective-permute-done | bytes 98336 | tf_op jit(solution)/shard_map/ppermute | solution.py:208
  16.5 1.5 %shard_map.33 = bf16[192,1024]{1,0:T(8,128)(2,1)} custom-call(bf16[1536,128]{1,0:T(8,128)(2,1)S(1)} %get-tuple-element.16.refs_0_, bf16[2,192,128]{2,1,0:T(8,128)(2,1)S(1)} %broadcast_select_fusion.1.refs_1_, f32[1,1536]{1,0:T(1,128)S(1)} %get-tuple-element.24.refs_2_, f32[1,1536]{1,0:T(1,128)S(1)} %get-tuple-element.25.refs_3_, ...), custom_call_target="tpu_custom_call" | custom-call | flops 150994944 | tf_op jit(solution)/shard_map/pallas_call | solution.py:155
  (5 shorter events, 0.1 us)
Async XLA Ops:
  0.0 4.7 %collective-permute-start = (bf16[2,192,128]{2,1,0:T(8,128)(2,1)}, bf16[2,192,128]{2,1,0:T(8,128)(2,1)S(1)}, u32[]{:S(2)}, u32[]{:S(2)}) collective-permute-start(bf16[2,192,128]{2,1,0:T(8,128)(2,1)} %block_ref.1), channel_id=1, source_target_pairs={{0,8},{1,9},{2,10},{3,11},{4,12},{5,13},{6,14},{7,15},{8,0},{9,1},... | collective-permute-start | bytes 294920 | tf_op jit(solution)/shard_map/ppermute | solution.py:208
  1.3 3.6 %collective-permute-start.1 = (bf16[2,192,128]{2,1,0:T(8,128)(2,1)}, bf16[2,192,128]{2,1,0:T(8,128)(2,1)S(1)}, u32[]{:S(2)}, u32[]{:S(2)}) collective-permute-start(bf16[2,192,128]{2,1,0:T(8,128)(2,1)} %block_ref.1), channel_id=1, source_target_pairs={{0,24},{1,0},{2,3},{3,2},{4,5},{5,4},{6,7},{7,6},{8,9},{9,8},{10,1... | collective-permute-start | bytes 294920 | tf_op jit(solution)/shard_map/ppermute | solution.py:211
  2.3 2.8 %collective-permute-start.2 = (bf16[2,192,128]{2,1,0:T(8,128)(2,1)}, bf16[2,192,128]{2,1,0:T(8,128)(2,1)S(1)}, u32[]{:S(2)}, u32[]{:S(2)}) collective-permute-start(bf16[2,192,128]{2,1,0:T(8,128)(2,1)} %block_ref.1), channel_id=1, source_target_pairs={{0,16},{1,0},{2,3},{3,2},{4,5},{5,4},{6,7},{7,6},{8,9},{9,8},{10,1... | collective-permute-start | bytes 294920 | tf_op jit(solution)/shard_map/ppermute | solution.py:211
  2.3 4.1 %collective-permute-start.3 = (bf16[2,192,128]{2,1,0:T(8,128)(2,1)}, bf16[2,192,128]{2,1,0:T(8,128)(2,1)S(1)}, u32[]{:S(2)}, u32[]{:S(2)}) collective-permute-start(bf16[2,192,128]{2,1,0:T(8,128)(2,1)} %block_ref.1), channel_id=1, source_target_pairs={{0,4},{1,5},{2,6},{3,7},{4,0},{5,1},{6,2},{7,3},{8,12},{9,13},{10,... | collective-permute-start | bytes 294920 | tf_op jit(solution)/shard_map/ppermute | solution.py:208
  3.5 3.8 %collective-permute-start.4 = (bf16[2,192,128]{2,1,0:T(8,128)(2,1)}, bf16[2,192,128]{2,1,0:T(8,128)(2,1)S(1)}, u32[]{:S(2)}, u32[]{:S(2)}) collective-permute-start(bf16[2,192,128]{2,1,0:T(8,128)(2,1)} %block_ref.1), channel_id=1, source_target_pairs={{0,2},{1,3},{2,0},{3,1},{4,6},{5,7},{6,4},{7,5},{8,10},{9,11},{10,... | collective-permute-start | bytes 294920 | tf_op jit(solution)/shard_map/ppermute | solution.py:208
  4.7 0.9 %copy-start = (bf16[2,192,128]{2,1,0:T(8,128)(2,1)S(1)}, bf16[2,192,128]{2,1,0:T(8,128)(2,1)}, u32[]{:S(2)}) copy-start(bf16[2,192,128]{2,1,0:T(8,128)(2,1)} %block_ref.1) | copy-start | bytes 294916
  4.7 7.7 %collective-permute-start.8 = (bf16[2,192,128]{2,1,0:T(8,128)(2,1)}, bf16[2,192,128]{2,1,0:T(8,128)(2,1)S(1)}, u32[]{:S(2)}, u32[]{:S(2)}) collective-permute-start(bf16[2,192,128]{2,1,0:T(8,128)(2,1)} %block_ref.1), channel_id=1, source_target_pairs={{0,16},{1,17},{2,18},{3,19},{4,20},{5,21},{6,22},{7,23},{8,24},{9,... | collective-permute-start | bytes 294920 | tf_op jit(solution)/shard_map/ppermute | solution.py:208
  5.6 5.1 %copy-start.1 = (bf16[192,1024]{1,0:T(8,128)(2,1)S(1)}, bf16[192,1024]{1,0:T(8,128)(2,1)}, u32[]{:S(2)}) copy-start(bf16[192,1024]{1,0:T(8,128)(2,1)} %refs_0_.1) | copy-start | bytes 1179652
  7.4 5.9 %collective-permute-start.5 = (bf16[2,192,128]{2,1,0:T(8,128)(2,1)S(1)}, bf16[2,192,128]{2,1,0:T(8,128)(2,1)S(1)}, u32[]{:S(2)}, u32[]{:S(2)}) collective-permute-start(bf16[2,192,128]{2,1,0:T(8,128)(2,1)S(1)} %get-tuple-element.28), channel_id=1, source_target_pairs={{0,1},{1,0},{2,3},{3,2},{4,6},{5,4},{6,7},{7,5},{8,10},{9,8},{10,1... | collective-permute-start | bytes 294920 | tf_op jit(solution)/shard_map/ppermute | solution.py:211
  9.2 4.1 %collective-permute-start.6 = (bf16[2,192,128]{2,1,0:T(8,128)(2,1)S(1)}, bf16[2,192,128]{2,1,0:T(8,128)(2,1)S(1)}, u32[]{:S(2)}, u32[]{:S(2)}) collective-permute-start(bf16[2,192,128]{2,1,0:T(8,128)(2,1)S(1)} %shard_map.28.after_ref), channel_id=1, source_target_pairs={{0,1},{1,0},{2,3},{3,2},{4,5},{5,4},{6,7},{7,6},{8,12},{9,8},{10,1... | collective-permute-start | bytes 294920 | tf_op jit(solution)/shard_map/ppermute | solution.py:211
  10.7 4.4 %collective-permute-start.7 = (bf16[2,192,128]{2,1,0:T(8,128)(2,1)S(1)}, bf16[2,192,128]{2,1,0:T(8,128)(2,1)S(1)}, u32[]{:S(2)}, u32[]{:S(2)}) collective-permute-start(bf16[2,192,128]{2,1,0:T(8,128)(2,1)S(1)} %shard_map.28.after_ref), channel_id=1, source_target_pairs={{0,1},{1,0},{2,3},{3,2},{4,5},{5,4},{6,7},{7,6},{8,14},{9,8},{10,1... | collective-permute-start | bytes 294920 | tf_op jit(solution)/shard_map/ppermute | solution.py:211
  15.1 1.4 %collective-permute-start.9 = (bf16[2,192,128]{2,1,0:T(8,128)(2,1)S(1)}, bf16[2,192,128]{2,1,0:T(8,128)(2,1)S(1)}, u32[]{:S(2)}, u32[]{:S(2)}) collective-permute-start(bf16[2,192,128]{2,1,0:T(8,128)(2,1)S(1)} %get-tuple-element.30), channel_id=1, source_target_pairs={{0,1},{1,0},{2,3},{3,2},{4,5},{5,4},{6,7},{7,6},{8,9},{9,8},{10,11... | collective-permute-start | bytes 294920 | tf_op jit(solution)/shard_map/ppermute | solution.py:208

commit v4 on v3

--- a/solution.py
+++ b/solution.py
@@ -45,7 +45,7 @@
 
 def plan(seeds, later, count):
     slots = {s: list(range(FANOUT)) for s in seeds} | {s: [FANOUT - 1] for s in later}
-    holders = {0, *slots} | {1 << b for b in range(count.bit_length() - 1)}
+    holders = {0, *slots} | {1 << b for b in range(1, count.bit_length() - 1)}
     missing = [t for t in range(0, count, 2) if t not in holders]
     waves = []
     while missing:
@@ -211,32 +211,34 @@
         return lax.ppermute(value, AXIS, fill(real, count))
 
     received = {bit: swap(keyval, bit) for bit in range(1, levels)}
-    seeds = {high: received[levels - 2]}
-    seeds |= {holder: send(keyval, [(0, holder)]) for holder in (high | top, top)}
+    seeds = {holder: send(keyval, [(0, holder)]) for holder in (top, high | top)}
+    seeds = {top: seeds[top], high: received[levels - 2], high | top: seeds[high | top]}
     first = pick(seeds)
     own = hold(keyval, first)
     later = {4: received[2]}
     waves = plan(list(seeds), list(later), count)
     for k, wave in enumerate(waves):
-        came = []
-        for real in wave:
-            if k == 0 and real is wave[-1]:
-                for holder, got in (later | {0: own}).items():
-                    first = jnp.where(me == holder, got, first)
-            came.append((send(first, real), [t for _, t in real]))
+        filled = first
+        if k == 0:
+            for holder, got in (later | {0: own}).items():
+                filled = jnp.where(me == holder, got, filled)
+        came = [(send(filled, wave[-1]), [t for _, t in wave[-1]])]
+        came += [(send(first, real), [t for _, t in real]) for real in wave[-2::-1]]
+        first = filled
         if k == 0:
             for bit in range(1, levels - 2):
                 if 1 << bit not in later:
                     first = jnp.where(me == 1 << bit, received[bit], first)
             received[0] = jnp.where(me == top, seeds[high | top], seeds[top])
-            received[0] = jnp.where(me == 1, came[-1][0], received[0])
+            received[0] = jnp.where(me == 1, came[0][0], received[0])
         if k + 1 == len(waves):
-            *state, stacked = attend(queries, [own, *(received[bit] for bit in range(levels - 2, 0, -1))])
-            *state, first = attend(stacked, [received[levels - 1]], state, carry=first)
+            *state, stacked = attend(queries, [own, *(received[bit] for bit in range(levels - 2, 1, -1))])
+            *state, first = attend(stacked, [received[1]], state, carry=first)
+            first = hold(first, received[levels - 1])
         for got, holders in came:
             first = jnp.where(member(me, holders), got, first)
     passed = swap(first, 0)
-    state = attend(stacked, [received[0]], state)
+    state = attend(stacked, [received[levels - 1], received[0]], state)
     first = jnp.where(me % 2 == 1, passed, first)
     return attend(stacked, [first], state, last=True)[0]
 

time: 18.1 us -> 17.6 us (0.972)
  the two profiles are of different devices: /device:TPU:17 before, /device:TPU:23 now
where the time goes in v4:
time: 17.6 us; the launch traced here: 17.5 us
  starting transfers between devices  9.52 us (54%)
  Pallas kernels  4.95 us (28%)
  waiting for transfers between devices  2.81 us (16%)
    ppermute x5, starting transfers between devices, swap(): return lax.ppermute(value, AXIS, [(i, i ^ 1 << bit) for i in range(count)])  6.03 us
    pallas_call x4, Pallas kernels, attend(): pl.pallas_call(functools.partial(attend_body, len(blocks), state is None,...  4.93 us
    ppermute x5, starting transfers between devices, send(): return lax.ppermute(value, AXIS, fill(real, count))  3.49 us
    ppermute x5, waiting for transfers between devices, swap(): return lax.ppermute(value, AXIS, [(i, i ^ 1 << bit) for i in range(count)])  2.8 us
  transfers between devices with their start and end apart: 10, of which 2 were waited for; matrix products, arithmetic and copies ran while one was open for 0% of the time, Pallas kernels for 20%

profile of v4, /device:TPU:23, one launch (start us, length us, event | category | flops | bytes accessed | tf_op | source)
XLA Modules:
  0.0 17.5 jit_solution(11989383227702541460)
XLA Ops:
  0.0 0.7 %collective-permute-start = (bf16[2,192,128]{2,1,0:T(8,128)(2,1)}, bf16[2,192,128]{2,1,0:T(8,128)(2,1)S(1)}, u32[]{:S(2)}, u32[]{:S(2)}) collective-permute-start(bf16[2,192,128]{2,1,0:T(8,128)(2,1)} %block_ref.1), channel_id=1, source_target_pairs={{0,16},{1,0},{2,3},{3,2},{4,5},{5,4},{6,7},{7,6},{8,9},{9,8},{10,1... | collective-permute-start | bytes 294920 | tf_op jit(solution)/shard_map/ppermute | solution.py:211
  0.7 1.3 %collective-permute-start.1 = (bf16[2,192,128]{2,1,0:T(8,128)(2,1)}, bf16[2,192,128]{2,1,0:T(8,128)(2,1)S(1)}, u32[]{:S(2)}, u32[]{:S(2)}) collective-permute-start(bf16[2,192,128]{2,1,0:T(8,128)(2,1)} %block_ref.1), channel_id=1, source_target_pairs={{0,8},{1,9},{2,10},{3,11},{4,12},{5,13},{6,14},{7,15},{8,0},{9,1},... | collective-permute-start | bytes 294920 | tf_op jit(solution)/shard_map/ppermute | solution.py:208
  2.0 0.3 %collective-permute-start.2 = (bf16[2,192,128]{2,1,0:T(8,128)(2,1)}, bf16[2,192,128]{2,1,0:T(8,128)(2,1)S(1)}, u32[]{:S(2)}, u32[]{:S(2)}) collective-permute-start(bf16[2,192,128]{2,1,0:T(8,128)(2,1)} %block_ref.1), channel_id=1, source_target_pairs={{0,24},{1,0},{2,3},{3,2},{4,5},{5,4},{6,7},{7,6},{8,9},{9,8},{10,1... | collective-permute-start | bytes 294920 | tf_op jit(solution)/shard_map/ppermute | solution.py:211
  2.3 0.2 %collective-permute-start.3 = (bf16[2,192,128]{2,1,0:T(8,128)(2,1)}, bf16[2,192,128]{2,1,0:T(8,128)(2,1)S(1)}, u32[]{:S(2)}, u32[]{:S(2)}) collective-permute-start(bf16[2,192,128]{2,1,0:T(8,128)(2,1)} %block_ref.1), channel_id=1, source_target_pairs={{0,4},{1,5},{2,6},{3,7},{4,0},{5,1},{6,2},{7,3},{8,12},{9,13},{10,... | collective-permute-start | bytes 294920 | tf_op jit(solution)/shard_map/ppermute | solution.py:208
  2.5 0.3 %collective-permute-start.7 = (bf16[2,192,128]{2,1,0:T(8,128)(2,1)}, bf16[2,192,128]{2,1,0:T(8,128)(2,1)S(1)}, u32[]{:S(2)}, u32[]{:S(2)}) collective-permute-start(bf16[2,192,128]{2,1,0:T(8,128)(2,1)} %block_ref.1), channel_id=1, source_target_pairs={{0,2},{1,3},{2,0},{3,1},{4,6},{5,7},{6,4},{7,5},{8,10},{9,11},{10,... | collective-permute-start | bytes 294920 | tf_op jit(solution)/shard_map/ppermute | solution.py:208
  2.7 0.0 copy-start
  2.7 0.0 collective-permute-done.refs_0_
  2.7 1.1 %collective-permute-start.8 = (bf16[2,192,128]{2,1,0:T(8,128)(2,1)}, bf16[2,192,128]{2,1,0:T(8,128)(2,1)S(1)}, u32[]{:S(2)}, u32[]{:S(2)}) collective-permute-start(bf16[2,192,128]{2,1,0:T(8,128)(2,1)} %block_ref.1), channel_id=1, source_target_pairs={{0,16},{1,17},{2,18},{3,19},{4,20},{5,21},{6,22},{7,23},{8,24},{9,... | collective-permute-start | bytes 294920 | tf_op jit(solution)/shard_map/ppermute | solution.py:208
  3.8 1.5 %collective-permute-done.1.refs_1_.refs_2_ = bf16[2,192,128]{2,1,0:T(8,128)(2,1)S(1)} collective-permute-done((bf16[2,192,128]{2,1,0:T(8,128)(2,1)}, bf16[2,192,128]{2,1,0:T(8,128)(2,1)S(1)}, u32[]{:S(2)}, u32[]{:S(2)}) %collective-permute-start.1) | collective-permute-done | bytes 98336 | tf_op jit(solution)/shard_map/ppermute | solution.py:208
  5.3 0.0 collective-permute-done.2.refs_2_
  5.3 0.0 copy-done
  5.3 0.0 copy-start.1
  5.3 1.3 %collective-permute-done.3.refs_3_ = bf16[2,192,128]{2,1,0:T(8,128)(2,1)S(1)} collective-permute-done((bf16[2,192,128]{2,1,0:T(8,128)(2,1)}, bf16[2,192,128]{2,1,0:T(8,128)(2,1)S(1)}, u32[]{:S(2)}, u32[]{:S(2)}) %collective-permute-start.3) | collective-permute-done | bytes 98336 | tf_op jit(solution)/shard_map/ppermute | solution.py:208
  6.6 0.0 collective-permute-done.7.refs_1_
  6.7 1.3 %collective-permute-start.6 = (bf16[2,192,128]{2,1,0:T(8,128)(2,1)S(1)}, bf16[2,192,128]{2,1,0:T(8,128)(2,1)S(1)}, u32[]{:S(2)}, u32[]{:S(2)}) collective-permute-start(bf16[2,192,128]{2,1,0:T(8,128)(2,1)S(1)} %get-tuple-element.28), channel_id=1, source_target_pairs={{0,1},{1,0},{2,3},{3,2},{4,6},{5,4},{6,7},{7,5},{8,10},{9,8},{10,1... | collective-permute-start | bytes 294920 | tf_op jit(solution)/shard_map/ppermute | solution.py:211
  8.0 1.2 %collective-permute-start.4 = (bf16[2,192,128]{2,1,0:T(8,128)(2,1)S(1)}, bf16[2,192,128]{2,1,0:T(8,128)(2,1)S(1)}, u32[]{:S(2)}, u32[]{:S(2)}) collective-permute-start(bf16[2,192,128]{2,1,0:T(8,128)(2,1)S(1)} %shard_map.28.after_ref), channel_id=1, source_target_pairs={{0,1},{1,0},{2,3},{3,2},{4,5},{5,4},{6,7},{7,6},{8,14},{9,8},{10,1... | collective-permute-start | bytes 294920 | tf_op jit(solution)/shard_map/ppermute | solution.py:211
  9.2 0.0 collective-permute-start.5
  9.2 0.0 copy-done.1
  9.2 1.4 %shard_map.30 = (f32[1,1536]{1,0:T(1,128)S(1)}, f32[1,1536]{1,0:T(1,128)S(1)}, f32[128,1536]{1,0:T(8,128)S(1)}, bf16[1536,128]{1,0:T(8,128)(2,1)S(1)}) custom-call(bf16[192,1024]{1,0:T(8,128)(2,1)S(1)} %copy-done.1, bf16[2,192,128]{2,1,0:T(8,128)(2,1)S(1)} %shard_map.29.refs_1_, bf16[2,192,128]{2,1,0:T(8,128)(2,1)S(1)} %collective-permute-done.1.refs_1_.refs_2_, ...), custom_call_target="tpu_custom_call" | custom-call | flops 452984832 | tf_op jit(solution)/shard_map/pallas_call | solution.py:155
  10.6 0.8 %shard_map.31 = (f32[1,1536]{1,0:T(1,128)S(1)}, f32[1,1536]{1,0:T(1,128)S(1)}, f32[128,1536]{1,0:T(8,128)S(1)}, bf16[2,192,128]{2,1,0:T(8,128)(2,1)S(1)}) custom-call(bf16[1536,128]{1,0:T(8,128)(2,1)S(1)} %get-tuple-element.16.refs_0_, bf16[2,192,128]{2,1,0:T(8,128)(2,1)S(1)} %collective-permute-done.7.refs_1_, f32[1,1536]{1,0:T(1,128)S(1)} %get-tuple-element.17.refs_2_, ...), custom_call_target="tpu_custom_call" | custom-call | flops 150994944 | tf_op jit(solution)/shard_map/pallas_call | solution.py:155
  11.4 0.0 collective-permute-done.8.after_ref.refs_1_
  11.5 0.0 collective-permute-done.6
  11.5 0.0 collective-permute-done.4
  11.5 0.0 collective-permute-done.5
  11.5 3.2 %collective-permute-start.9 = (bf16[2,192,128]{2,1,0:T(8,128)(2,1)S(1)}, bf16[2,192,128]{2,1,0:T(8,128)(2,1)S(1)}, u32[]{:S(2)}, u32[]{:S(2)}) collective-permute-start(bf16[2,192,128]{2,1,0:T(8,128)(2,1)S(1)} %get-tuple-element.30), channel_id=1, source_target_pairs={{0,1},{1,0},{2,3},{3,2},{4,5},{5,4},{6,7},{7,6},{8,9},{9,8},{10,11... | collective-permute-start | bytes 294920 | tf_op jit(solution)/shard_map/ppermute | solution.py:208
  14.7 1.2 %shard_map.33 = (f32[1,1536]{1,0:T(1,128)S(1)}, f32[1,1536]{1,0:T(1,128)S(1)}, f32[128,1536]{1,0:T(8,128)S(1)}) custom-call(bf16[1536,128]{1,0:T(8,128)(2,1)S(1)} %get-tuple-element.16.refs_0_, bf16[2,192,128]{2,1,0:T(8,128)(2,1)S(1)} %collective-permute-done.8.after_ref.refs_1_, bf16[2,192,128]{2,1,0:T(8,128)(2,1)S(1)} %get-tuple-element.29.refs_2_, ...), custom_call_target="tpu_custom_call" | custom-call | flops 301989888 | tf_op jit(solution)/shard_map/pallas_call | solution.py:155
  16.0 0.0 collective-permute-done.9
  16.0 1.5 %shard_map.34 = bf16[192,1024]{1,0:T(8,128)(2,1)} custom-call(bf16[1536,128]{1,0:T(8,128)(2,1)S(1)} %get-tuple-element.16.refs_0_, bf16[2,192,128]{2,1,0:T(8,128)(2,1)S(1)} %broadcast_select_fusion.1.refs_1_, f32[1,1536]{1,0:T(1,128)S(1)} %get-tuple-element.24.refs_2_, f32[1,1536]{1,0:T(1,128)S(1)} %get-tuple-element.25.refs_3_, ...), custom_call_target="tpu_custom_call" | custom-call | flops 150994944 | tf_op jit(solution)/shard_map/pallas_call | solution.py:155
  (6 shorter events, 0.1 us)
Async XLA Ops:
  0.0 2.7 %collective-permute-start = (bf16[2,192,128]{2,1,0:T(8,128)(2,1)}, bf16[2,192,128]{2,1,0:T(8,128)(2,1)S(1)}, u32[]{:S(2)}, u32[]{:S(2)}) collective-permute-start(bf16[2,192,128]{2,1,0:T(8,128)(2,1)} %block_ref.1), channel_id=1, source_target_pairs={{0,16},{1,0},{2,3},{3,2},{4,5},{5,4},{6,7},{7,6},{8,9},{9,8},{10,1... | collective-permute-start | bytes 294920 | tf_op jit(solution)/shard_map/ppermute | solution.py:211
  0.7 4.6 %collective-permute-start.1 = (bf16[2,192,128]{2,1,0:T(8,128)(2,1)}, bf16[2,192,128]{2,1,0:T(8,128)(2,1)S(1)}, u32[]{:S(2)}, u32[]{:S(2)}) collective-permute-start(bf16[2,192,128]{2,1,0:T(8,128)(2,1)} %block_ref.1), channel_id=1, source_target_pairs={{0,8},{1,9},{2,10},{3,11},{4,12},{5,13},{6,14},{7,15},{8,0},{9,1},... | collective-permute-start | bytes 294920 | tf_op jit(solution)/shard_map/ppermute | solution.py:208
  2.0 3.3 %collective-permute-start.2 = (bf16[2,192,128]{2,1,0:T(8,128)(2,1)}, bf16[2,192,128]{2,1,0:T(8,128)(2,1)S(1)}, u32[]{:S(2)}, u32[]{:S(2)}) collective-permute-start(bf16[2,192,128]{2,1,0:T(8,128)(2,1)} %block_ref.1), channel_id=1, source_target_pairs={{0,24},{1,0},{2,3},{3,2},{4,5},{5,4},{6,7},{7,6},{8,9},{9,8},{10,1... | collective-permute-start | bytes 294920 | tf_op jit(solution)/shard_map/ppermute | solution.py:211
  2.3 4.4 %collective-permute-start.3 = (bf16[2,192,128]{2,1,0:T(8,128)(2,1)}, bf16[2,192,128]{2,1,0:T(8,128)(2,1)S(1)}, u32[]{:S(2)}, u32[]{:S(2)}) collective-permute-start(bf16[2,192,128]{2,1,0:T(8,128)(2,1)} %block_ref.1), channel_id=1, source_target_pairs={{0,4},{1,5},{2,6},{3,7},{4,0},{5,1},{6,2},{7,3},{8,12},{9,13},{10,... | collective-permute-start | bytes 294920 | tf_op jit(solution)/shard_map/ppermute | solution.py:208
  2.5 4.2 %collective-permute-start.7 = (bf16[2,192,128]{2,1,0:T(8,128)(2,1)}, bf16[2,192,128]{2,1,0:T(8,128)(2,1)S(1)}, u32[]{:S(2)}, u32[]{:S(2)}) collective-permute-start(bf16[2,192,128]{2,1,0:T(8,128)(2,1)} %block_ref.1), channel_id=1, source_target_pairs={{0,2},{1,3},{2,0},{3,1},{4,6},{5,7},{6,4},{7,5},{8,10},{9,11},{10,... | collective-permute-start | bytes 294920 | tf_op jit(solution)/shard_map/ppermute | solution.py:208
  2.7 2.6 %copy-start = (bf16[2,192,128]{2,1,0:T(8,128)(2,1)S(1)}, bf16[2,192,128]{2,1,0:T(8,128)(2,1)}, u32[]{:S(2)}) copy-start(bf16[2,192,128]{2,1,0:T(8,128)(2,1)} %block_ref.1) | copy-start | bytes 294916
  2.7 8.7 %collective-permute-start.8 = (bf16[2,192,128]{2,1,0:T(8,128)(2,1)}, bf16[2,192,128]{2,1,0:T(8,128)(2,1)S(1)}, u32[]{:S(2)}, u32[]{:S(2)}) collective-permute-start(bf16[2,192,128]{2,1,0:T(8,128)(2,1)} %block_ref.1), channel_id=1, source_target_pairs={{0,16},{1,17},{2,18},{3,19},{4,20},{5,21},{6,22},{7,23},{8,24},{9,... | collective-permute-start | bytes 294920 | tf_op jit(solution)/shard_map/ppermute | solution.py:208
  5.3 3.9 %copy-start.1 = (bf16[192,1024]{1,0:T(8,128)(2,1)S(1)}, bf16[192,1024]{1,0:T(8,128)(2,1)}, u32[]{:S(2)}) copy-start(bf16[192,1024]{1,0:T(8,128)(2,1)} %refs_0_.1) | copy-start | bytes 1179652
  6.7 4.8 %collective-permute-start.6 = (bf16[2,192,128]{2,1,0:T(8,128)(2,1)S(1)}, bf16[2,192,128]{2,1,0:T(8,128)(2,1)S(1)}, u32[]{:S(2)}, u32[]{:S(2)}) collective-permute-start(bf16[2,192,128]{2,1,0:T(8,128)(2,1)S(1)} %get-tuple-element.28), channel_id=1, source_target_pairs={{0,1},{1,0},{2,3},{3,2},{4,6},{5,4},{6,7},{7,5},{8,10},{9,8},{10,1... | collective-permute-start | bytes 294920 | tf_op jit(solution)/shard_map/ppermute | solution.py:211
  8.0 3.5 %collective-permute-start.4 = (bf16[2,192,128]{2,1,0:T(8,128)(2,1)S(1)}, bf16[2,192,128]{2,1,0:T(8,128)(2,1)S(1)}, u32[]{:S(2)}, u32[]{:S(2)}) collective-permute-start(bf16[2,192,128]{2,1,0:T(8,128)(2,1)S(1)} %shard_map.28.after_ref), channel_id=1, source_target_pairs={{0,1},{1,0},{2,3},{3,2},{4,5},{5,4},{6,7},{7,6},{8,14},{9,8},{10,1... | collective-permute-start | bytes 294920 | tf_op jit(solution)/shard_map/ppermute | solution.py:211
  9.2 2.3 %collective-permute-start.5 = (bf16[2,192,128]{2,1,0:T(8,128)(2,1)S(1)}, bf16[2,192,128]{2,1,0:T(8,128)(2,1)S(1)}, u32[]{:S(2)}, u32[]{:S(2)}) collective-permute-start(bf16[2,192,128]{2,1,0:T(8,128)(2,1)S(1)} %shard_map.28.after_ref), channel_id=1, source_target_pairs={{0,1},{1,0},{2,3},{3,2},{4,5},{5,4},{6,7},{7,6},{8,12},{9,8},{10,1... | collective-permute-start | bytes 294920 | tf_op jit(solution)/shard_map/ppermute | solution.py:211
  11.5 4.4 %collective-permute-start.9 = (bf16[2,192,128]{2,1,0:T(8,128)(2,1)S(1)}, bf16[2,192,128]{2,1,0:T(8,128)(2,1)S(1)}, u32[]{:S(2)}, u32[]{:S(2)}) collective-permute-start(bf16[2,192,128]{2,1,0:T(8,128)(2,1)S(1)} %get-tuple-element.30), channel_id=1, source_target_pairs={{0,1},{1,0},{2,3},{3,2},{4,5},{5,4},{6,7},{7,6},{8,9},{9,8},{10,11... | collective-permute-start | bytes 294920 | tf_op jit(solution)/shard_map/ppermute | solution.py:208

commit v5 on v4

--- a/solution.py
+++ b/solution.py
@@ -158,7 +158,7 @@
         in_specs=[VMEM] * len(args),
         out_specs=(VMEM,) * len(out_shape),
         compiler_params=pltpu.CompilerParams(vmem_limit_bytes=24 << 20),
-        cost_estimate=pl.CostEstimate(flops=4 * pairs * HD, bytes_accessed=0, transcendentals=pairs),
+        cost_estimate=pl.CostEstimate(flops=40 * pairs * HD, bytes_accessed=0, transcendentals=pairs),
     )(*args)
 
 

time: 17.6 us -> 17.1 us (0.972)
  the two profiles are of different devices: /device:TPU:23 before, /device:TPU:1 now
where the time goes in v5:
time: 17.1 us; the launch traced here: 17 us
  starting transfers between devices  9.79 us (57%)
  Pallas kernels  4.95 us (29%)
  waiting for transfers between devices  2.06 us (12%)
    ppermute x5, starting transfers between devices, swap(): return lax.ppermute(value, AXIS, [(i, i ^ 1 << bit) for i in range(count)])  7.05 us
    pallas_call x4, Pallas kernels, attend(): pl.pallas_call(functools.partial(attend_body, len(blocks), state is None,...  4.94 us
    ppermute x5, starting transfers between devices, send(): return lax.ppermute(value, AXIS, fill(real, count))  2.74 us
    ppermute x5, waiting for transfers between devices, send(): return lax.ppermute(value, AXIS, fill(real, count))  1.41 us
    ppermute x5, waiting for transfers between devices, swap(): return lax.ppermute(value, AXIS, [(i, i ^ 1 << bit) for i in range(count)])  0.65 us
  transfers between devices with their start and end apart: 10, of which 2 were waited for; matrix products, arithmetic and copies ran while one was open for 0% of the time, Pallas kernels for 20%

profile of v5, /device:TPU:1, one launch (start us, length us, event | category | flops | bytes accessed | tf_op | source)
XLA Modules:
  0.0 17.0 jit_solution(10287227320861146902)
XLA Ops:
  0.0 0.1 collective-permute-start
  0.1 2.7 %collective-permute-start.1 = (bf16[2,192,128]{2,1,0:T(8,128)(2,1)}, bf16[2,192,128]{2,1,0:T(8,128)(2,1)S(1)}, u32[]{:S(2)}, u32[]{:S(2)}) collective-permute-start(bf16[2,192,128]{2,1,0:T(8,128)(2,1)} %block_ref.1), channel_id=1, source_target_pairs={{0,8},{1,9},{2,10},{3,11},{4,12},{5,13},{6,14},{7,15},{8,0},{9,1},... | collective-permute-start | bytes 294920 | tf_op jit(solution)/shard_map/ppermute | solution.py:208
  2.8 1.3 %collective-permute-start.2 = (bf16[2,192,128]{2,1,0:T(8,128)(2,1)}, bf16[2,192,128]{2,1,0:T(8,128)(2,1)S(1)}, u32[]{:S(2)}, u32[]{:S(2)}) collective-permute-start(bf16[2,192,128]{2,1,0:T(8,128)(2,1)} %block_ref.1), channel_id=1, source_target_pairs={{0,24},{1,0},{2,3},{3,2},{4,5},{5,4},{6,7},{7,6},{8,9},{9,8},{10,1... | collective-permute-start | bytes 294920 | tf_op jit(solution)/shard_map/ppermute | solution.py:211
  4.1 0.2 %collective-permute-start.3 = (bf16[2,192,128]{2,1,0:T(8,128)(2,1)}, bf16[2,192,128]{2,1,0:T(8,128)(2,1)S(1)}, u32[]{:S(2)}, u32[]{:S(2)}) collective-permute-start(bf16[2,192,128]{2,1,0:T(8,128)(2,1)} %block_ref.1), channel_id=1, source_target_pairs={{0,4},{1,5},{2,6},{3,7},{4,0},{5,1},{6,2},{7,3},{8,12},{9,13},{10,... | collective-permute-start | bytes 294920 | tf_op jit(solution)/shard_map/ppermute | solution.py:208
  4.3 1.2 %collective-permute-start.7 = (bf16[2,192,128]{2,1,0:T(8,128)(2,1)}, bf16[2,192,128]{2,1,0:T(8,128)(2,1)S(1)}, u32[]{:S(2)}, u32[]{:S(2)}) collective-permute-start(bf16[2,192,128]{2,1,0:T(8,128)(2,1)} %block_ref.1), channel_id=1, source_target_pairs={{0,2},{1,3},{2,0},{3,1},{4,6},{5,7},{6,4},{7,5},{8,10},{9,11},{10,... | collective-permute-start | bytes 294920 | tf_op jit(solution)/shard_map/ppermute | solution.py:208
  5.5 0.0 copy-start
  5.5 0.0 collective-permute-done.refs_0_
  5.5 2.3 %collective-permute-start.8 = (bf16[2,192,128]{2,1,0:T(8,128)(2,1)}, bf16[2,192,128]{2,1,0:T(8,128)(2,1)S(1)}, u32[]{:S(2)}, u32[]{:S(2)}) collective-permute-start(bf16[2,192,128]{2,1,0:T(8,128)(2,1)} %block_ref.1), channel_id=1, source_target_pairs={{0,16},{1,17},{2,18},{3,19},{4,20},{5,21},{6,22},{7,23},{8,24},{9,... | collective-permute-start | bytes 294920 | tf_op jit(solution)/shard_map/ppermute | solution.py:208
  7.9 0.0 collective-permute-done.1.refs_1_.refs_2_
  7.9 1.4 %collective-permute-done.2.refs_2_ = bf16[2,192,128]{2,1,0:T(8,128)(2,1)S(1)} collective-permute-done((bf16[2,192,128]{2,1,0:T(8,128)(2,1)}, bf16[2,192,128]{2,1,0:T(8,128)(2,1)S(1)}, u32[]{:S(2)}, u32[]{:S(2)}) %collective-permute-start.2) | collective-permute-done | bytes 98336 | tf_op jit(solution)/shard_map/ppermute | solution.py:211
  9.3 0.0 copy-done
  9.3 0.0 copy-start.1
  9.3 0.8 %collective-permute-start.4 = (bf16[2,192,128]{2,1,0:T(8,128)(2,1)S(1)}, bf16[2,192,128]{2,1,0:T(8,128)(2,1)S(1)}, u32[]{:S(2)}, u32[]{:S(2)}) collective-permute-start(bf16[2,192,128]{2,1,0:T(8,128)(2,1)S(1)} %shard_map.28.after_ref), channel_id=1, source_target_pairs={{0,1},{1,0},{2,3},{3,2},{4,5},{5,4},{6,7},{7,6},{8,14},{9,8},{10,1... | collective-permute-start | bytes 294920 | tf_op jit(solution)/shard_map/ppermute | solution.py:211
  10.1 0.1 collective-permute-start.5
  10.2 0.0 collective-permute-done.3.refs_3_
  10.2 0.0 collective-permute-done.7.refs_1_
  10.2 0.5 %collective-permute-start.6 = (bf16[2,192,128]{2,1,0:T(8,128)(2,1)S(1)}, bf16[2,192,128]{2,1,0:T(8,128)(2,1)S(1)}, u32[]{:S(2)}, u32[]{:S(2)}) collective-permute-start(bf16[2,192,128]{2,1,0:T(8,128)(2,1)S(1)} %get-tuple-element.28), channel_id=1, source_target_pairs={{0,1},{1,0},{2,3},{3,2},{4,6},{5,4},{6,7},{7,5},{8,10},{9,8},{10,1... | collective-permute-start | bytes 294920 | tf_op jit(solution)/shard_map/ppermute | solution.py:211
  10.7 0.0 copy-done.1
  10.7 1.4 %shard_map.30 = (f32[1,1536]{1,0:T(1,128)S(1)}, f32[1,1536]{1,0:T(1,128)S(1)}, f32[128,1536]{1,0:T(8,128)S(1)}, bf16[1536,128]{1,0:T(8,128)(2,1)S(1)}) custom-call(bf16[192,1024]{1,0:T(8,128)(2,1)S(1)} %copy-done.1, bf16[2,192,128]{2,1,0:T(8,128)(2,1)S(1)} %shard_map.29.refs_1_, bf16[2,192,128]{2,1,0:T(8,128)(2,1)S(1)} %collective-permute-done.1.refs_1_.refs_2_, ...), custom_call_target="tpu_custom_call" | custom-call | flops 4529848320 | tf_op jit(solution)/shard_map/pallas_call | solution.py:155
  12.1 0.8 %shard_map.31 = (f32[1,1536]{1,0:T(1,128)S(1)}, f32[1,1536]{1,0:T(1,128)S(1)}, f32[128,1536]{1,0:T(8,128)S(1)}, bf16[2,192,128]{2,1,0:T(8,128)(2,1)S(1)}) custom-call(bf16[1536,128]{1,0:T(8,128)(2,1)S(1)} %get-tuple-element.16.refs_0_, bf16[2,192,128]{2,1,0:T(8,128)(2,1)S(1)} %collective-permute-done.7.refs_1_, f32[1,1536]{1,0:T(1,128)S(1)} %get-tuple-element.17.refs_2_, ...), custom_call_target="tpu_custom_call" | custom-call | flops 1509949440 | tf_op jit(solution)/shard_map/pallas_call | solution.py:155
  12.9 0.6 %collective-permute-done.8.after_ref.refs_1_ = bf16[2,192,128]{2,1,0:T(8,128)(2,1)S(1)} collective-permute-done((bf16[2,192,128]{2,1,0:T(8,128)(2,1)}, bf16[2,192,128]{2,1,0:T(8,128)(2,1)S(1)}, u32[]{:S(2)}, u32[]{:S(2)}) %collective-permute-start.8) | collective-permute-done | bytes 98336 | tf_op jit(solution)/shard_map/ppermute | solution.py:208
  13.6 0.0 collective-permute-done.6
  13.6 0.0 collective-permute-done.4
  13.6 0.0 collective-permute-done.5
  13.6 0.6 %collective-permute-start.9 = (bf16[2,192,128]{2,1,0:T(8,128)(2,1)S(1)}, bf16[2,192,128]{2,1,0:T(8,128)(2,1)S(1)}, u32[]{:S(2)}, u32[]{:S(2)}) collective-permute-start(bf16[2,192,128]{2,1,0:T(8,128)(2,1)S(1)} %get-tuple-element.30), channel_id=1, source_target_pairs={{0,1},{1,0},{2,3},{3,2},{4,5},{5,4},{6,7},{7,6},{8,9},{9,8},{10,11... | collective-permute-start | bytes 294920 | tf_op jit(solution)/shard_map/ppermute | solution.py:208
  14.2 1.2 %shard_map.33 = (f32[1,1536]{1,0:T(1,128)S(1)}, f32[1,1536]{1,0:T(1,128)S(1)}, f32[128,1536]{1,0:T(8,128)S(1)}) custom-call(bf16[1536,128]{1,0:T(8,128)(2,1)S(1)} %get-tuple-element.16.refs_0_, bf16[2,192,128]{2,1,0:T(8,128)(2,1)S(1)} %collective-permute-done.8.after_ref.refs_1_, bf16[2,192,128]{2,1,0:T(8,128)(2,1)S(1)} %get-tuple-element.29.refs_2_, ...), custom_call_target="tpu_custom_call" | custom-call | flops 3019898880 | tf_op jit(solution)/shard_map/pallas_call | solution.py:155
  15.5 0.0 collective-permute-done.9
  15.5 1.5 %shard_map.34 = bf16[192,1024]{1,0:T(8,128)(2,1)} custom-call(bf16[1536,128]{1,0:T(8,128)(2,1)S(1)} %get-tuple-element.16.refs_0_, bf16[2,192,128]{2,1,0:T(8,128)(2,1)S(1)} %broadcast_select_fusion.1.refs_1_, f32[1,1536]{1,0:T(1,128)S(1)} %get-tuple-element.24.refs_2_, f32[1,1536]{1,0:T(1,128)S(1)} %get-tuple-element.25.refs_3_, ...), custom_call_target="tpu_custom_call" | custom-call | flops 1509949440 | tf_op jit(solution)/shard_map/pallas_call | solution.py:155
  (6 shorter events, 0.1 us)
Async XLA Ops:
  0.0 5.5 %collective-permute-start = (bf16[2,192,128]{2,1,0:T(8,128)(2,1)}, bf16[2,192,128]{2,1,0:T(8,128)(2,1)S(1)}, u32[]{:S(2)}, u32[]{:S(2)}) collective-permute-start(bf16[2,192,128]{2,1,0:T(8,128)(2,1)} %block_ref.1), channel_id=1, source_target_pairs={{0,16},{1,0},{2,3},{3,2},{4,5},{5,4},{6,7},{7,6},{8,9},{9,8},{10,1... | collective-permute-start | bytes 294920 | tf_op jit(solution)/shard_map/ppermute | solution.py:211
  0.1 7.8 %collective-permute-start.1 = (bf16[2,192,128]{2,1,0:T(8,128)(2,1)}, bf16[2,192,128]{2,1,0:T(8,128)(2,1)S(1)}, u32[]{:S(2)}, u32[]{:S(2)}) collective-permute-start(bf16[2,192,128]{2,1,0:T(8,128)(2,1)} %block_ref.1), channel_id=1, source_target_pairs={{0,8},{1,9},{2,10},{3,11},{4,12},{5,13},{6,14},{7,15},{8,0},{9,1},... | collective-permute-start | bytes 294920 | tf_op jit(solution)/shard_map/ppermute | solution.py:208
  2.8 6.5 %collective-permute-start.2 = (bf16[2,192,128]{2,1,0:T(8,128)(2,1)}, bf16[2,192,128]{2,1,0:T(8,128)(2,1)S(1)}, u32[]{:S(2)}, u32[]{:S(2)}) collective-permute-start(bf16[2,192,128]{2,1,0:T(8,128)(2,1)} %block_ref.1), channel_id=1, source_target_pairs={{0,24},{1,0},{2,3},{3,2},{4,5},{5,4},{6,7},{7,6},{8,9},{9,8},{10,1... | collective-permute-start | bytes 294920 | tf_op jit(solution)/shard_map/ppermute | solution.py:211
  4.1 6.1 %collective-permute-start.3 = (bf16[2,192,128]{2,1,0:T(8,128)(2,1)}, bf16[2,192,128]{2,1,0:T(8,128)(2,1)S(1)}, u32[]{:S(2)}, u32[]{:S(2)}) collective-permute-start(bf16[2,192,128]{2,1,0:T(8,128)(2,1)} %block_ref.1), channel_id=1, source_target_pairs={{0,4},{1,5},{2,6},{3,7},{4,0},{5,1},{6,2},{7,3},{8,12},{9,13},{10,... | collective-permute-start | bytes 294920 | tf_op jit(solution)/shard_map/ppermute | solution.py:208
  4.3 5.8 %collective-permute-start.7 = (bf16[2,192,128]{2,1,0:T(8,128)(2,1)}, bf16[2,192,128]{2,1,0:T(8,128)(2,1)S(1)}, u32[]{:S(2)}, u32[]{:S(2)}) collective-permute-start(bf16[2,192,128]{2,1,0:T(8,128)(2,1)} %block_ref.1), channel_id=1, source_target_pairs={{0,2},{1,3},{2,0},{3,1},{4,6},{5,7},{6,4},{7,5},{8,10},{9,11},{10,... | collective-permute-start | bytes 294920 | tf_op jit(solution)/shard_map/ppermute | solution.py:208
  5.5 3.7 %copy-start = (bf16[2,192,128]{2,1,0:T(8,128)(2,1)S(1)}, bf16[2,192,128]{2,1,0:T(8,128)(2,1)}, u32[]{:S(2)}) copy-start(bf16[2,192,128]{2,1,0:T(8,128)(2,1)} %block_ref.1) | copy-start | bytes 294916
  5.5 8.0 %collective-permute-start.8 = (bf16[2,192,128]{2,1,0:T(8,128)(2,1)}, bf16[2,192,128]{2,1,0:T(8,128)(2,1)S(1)}, u32[]{:S(2)}, u32[]{:S(2)}) collective-permute-start(bf16[2,192,128]{2,1,0:T(8,128)(2,1)} %block_ref.1), channel_id=1, source_target_pairs={{0,16},{1,17},{2,18},{3,19},{4,20},{5,21},{6,22},{7,23},{8,24},{9,... | collective-permute-start | bytes 294920 | tf_op jit(solution)/shard_map/ppermute | solution.py:208
  9.3 1.4 %copy-start.1 = (bf16[192,1024]{1,0:T(8,128)(2,1)S(1)}, bf16[192,1024]{1,0:T(8,128)(2,1)}, u32[]{:S(2)}) copy-start(bf16[192,1024]{1,0:T(8,128)(2,1)} %refs_0_.1) | copy-start | bytes 1179652
  9.3 4.3 %collective-permute-start.4 = (bf16[2,192,128]{2,1,0:T(8,128)(2,1)S(1)}, bf16[2,192,128]{2,1,0:T(8,128)(2,1)S(1)}, u32[]{:S(2)}, u32[]{:S(2)}) collective-permute-start(bf16[2,192,128]{2,1,0:T(8,128)(2,1)S(1)} %shard_map.28.after_ref), channel_id=1, source_target_pairs={{0,1},{1,0},{2,3},{3,2},{4,5},{5,4},{6,7},{7,6},{8,14},{9,8},{10,1... | collective-permute-start | bytes 294920 | tf_op jit(solution)/shard_map/ppermute | solution.py:211
  10.1 3.5 %collective-permute-start.5 = (bf16[2,192,128]{2,1,0:T(8,128)(2,1)S(1)}, bf16[2,192,128]{2,1,0:T(8,128)(2,1)S(1)}, u32[]{:S(2)}, u32[]{:S(2)}) collective-permute-start(bf16[2,192,128]{2,1,0:T(8,128)(2,1)S(1)} %shard_map.28.after_ref), channel_id=1, source_target_pairs={{0,1},{1,0},{2,3},{3,2},{4,5},{5,4},{6,7},{7,6},{8,12},{9,8},{10,1... | collective-permute-start | bytes 294920 | tf_op jit(solution)/shard_map/ppermute | solution.py:211
  10.2 3.4 %collective-permute-start.6 = (bf16[2,192,128]{2,1,0:T(8,128)(2,1)S(1)}, bf16[2,192,128]{2,1,0:T(8,128)(2,1)S(1)}, u32[]{:S(2)}, u32[]{:S(2)}) collective-permute-start(bf16[2,192,128]{2,1,0:T(8,128)(2,1)S(1)} %get-tuple-element.28), channel_id=1, source_target_pairs={{0,1},{1,0},{2,3},{3,2},{4,6},{5,4},{6,7},{7,5},{8,10},{9,8},{10,1... | collective-permute-start | bytes 294920 | tf_op jit(solution)/shard_map/ppermute | solution.py:211
  13.6 1.8 %collective-permute-start.9 = (bf16[2,192,128]{2,1,0:T(8,128)(2,1)S(1)}, bf16[2,192,128]{2,1,0:T(8,128)(2,1)S(1)}, u32[]{:S(2)}, u32[]{:S(2)}) collective-permute-start(bf16[2,192,128]{2,1,0:T(8,128)(2,1)S(1)} %get-tuple-element.30), channel_id=1, source_target_pairs={{0,1},{1,0},{2,3},{3,2},{4,5},{5,4},{6,7},{7,6},{8,9},{9,8},{10,11... | collective-permute-start | bytes 294920 | tf_op jit(solution)/shard_map/ppermute | solution.py:208

commit v6 on v5

--- a/solution.py
+++ b/solution.py
@@ -198,6 +198,11 @@
     )(*args)
 
 
+def way(target, side):
+    stops = [0, target, target ^ 1, target ^ side, target ^ side ^ 1, side ^ 1, side, 1, 0]
+    return list(zip(stops, stops[1:]))
+
+
 def on_device(queries, keyval):
     count = lax.axis_size(AXIS)
     levels = count.bit_length() - 1
@@ -211,7 +216,7 @@
         return lax.ppermute(value, AXIS, fill(real, count))
 
     received = {bit: swap(keyval, bit) for bit in range(1, levels)}
-    seeds = {holder: send(keyval, [(0, holder)]) for holder in (top, high | top)}
+    seeds = {holder: send(keyval, way(holder, side)) for holder, side in ((top, 4), (high | top, 2))}
     seeds = {top: seeds[top], high: received[levels - 2], high | top: seeds[high | top]}
     first = pick(seeds)
     own = hold(keyval, first)
@@ -229,7 +234,7 @@
             for bit in range(1, levels - 2):
                 if 1 << bit not in later:
                     first = jnp.where(me == 1 << bit, received[bit], first)
-            received[0] = jnp.where(me == top, seeds[high | top], seeds[top])
+            received[0] = jnp.where(member(me, [top, top ^ 4, 5]), seeds[high | top], seeds[top])
             received[0] = jnp.where(me == 1, came[0][0], received[0])
         if k + 1 == len(waves):
             *state, stacked = attend(queries, [own, *(received[bit] for bit in range(levels - 2, 1, -1))])

time: 17.1 us -> 17.1 us (level)
  waiting for transfers between devices: 2.06 us -> 0.68 us
  starting transfers between devices: 9.79 us -> 11.1 us
    ppermute x5, waiting for transfers between devices: 1.41 us -> 0.01 us  [send(): return lax.ppermute(value, AXIS, fill(real, count))]
    ppermute x5, starting transfers between devices: 2.74 us -> 3.94 us  [send(): return lax.ppermute(value, AXIS, fill(real, count))]
  transfers between devices with their start and end apart: 10 -> 10, of which waited for: 2 -> 1; matrix products, arithmetic and copies ran while one was open for 0% -> 0% of each run, Pallas kernels for 20% -> 21%
where the time goes in v6:
time: 17.1 us; the launch traced here: 16.9 us
  starting transfers between devices  11.1 us (65%)
  Pallas kernels  4.96 us (29%)
  waiting for transfers between devices  0.68 us (4%)
    ppermute x5, starting transfers between devices, swap(): return lax.ppermute(value, AXIS, [(i, i ^ 1 << bit) for i in range(count)])  7.14 us
    pallas_call x4, Pallas kernels, attend(): pl.pallas_call(functools.partial(attend_body, len(blocks), state is None,...  4.95 us
    ppermute x5, starting transfers between devices, send(): return lax.ppermute(value, AXIS, fill(real, count))  3.94 us
    ppermute x5, waiting for transfers between devices, swap(): return lax.ppermute(value, AXIS, [(i, i ^ 1 << bit) for i in range(count)])  0.66 us
  transfers between devices with their start and end apart: 10, of which 1 were waited for; matrix products, arithmetic and copies ran while one was open for 0% of the time, Pallas kernels for 21%

profile of v6, /device:TPU:1, one launch (start us, length us, event | category | flops | bytes accessed | tf_op | source)
XLA Modules:
  0.0 16.9 jit_solution(2480394350140905519)
XLA Ops:
  0.0 0.1 collective-permute-start
  0.1 2.7 %collective-permute-start.1 = (bf16[2,192,128]{2,1,0:T(8,128)(2,1)}, bf16[2,192,128]{2,1,0:T(8,128)(2,1)S(1)}, u32[]{:S(2)}, u32[]{:S(2)}) collective-permute-start(bf16[2,192,128]{2,1,0:T(8,128)(2,1)} %block_ref.1), channel_id=1, source_target_pairs={{0,8},{1,9},{2,10},{3,11},{4,12},{5,13},{6,14},{7,15},{8,0},{9,1},... | collective-permute-start | bytes 294920 | tf_op jit(solution)/shard_map/ppermute | solution.py:213
  2.8 1.3 %collective-permute-start.2 = (bf16[2,192,128]{2,1,0:T(8,128)(2,1)}, bf16[2,192,128]{2,1,0:T(8,128)(2,1)S(1)}, u32[]{:S(2)}, u32[]{:S(2)}) collective-permute-start(bf16[2,192,128]{2,1,0:T(8,128)(2,1)} %block_ref.1), channel_id=1, source_target_pairs={{0,24},{1,0},{2,1},{3,2},{4,5},{5,4},{6,7},{7,6},{8,9},{9,8},{10,1... | collective-permute-start | bytes 294920 | tf_op jit(solution)/shard_map/ppermute | solution.py:216
  4.1 0.2 %collective-permute-start.3 = (bf16[2,192,128]{2,1,0:T(8,128)(2,1)}, bf16[2,192,128]{2,1,0:T(8,128)(2,1)S(1)}, u32[]{:S(2)}, u32[]{:S(2)}) collective-permute-start(bf16[2,192,128]{2,1,0:T(8,128)(2,1)} %block_ref.1), channel_id=1, source_target_pairs={{0,4},{1,5},{2,6},{3,7},{4,0},{5,1},{6,2},{7,3},{8,12},{9,13},{10,... | collective-permute-start | bytes 294920 | tf_op jit(solution)/shard_map/ppermute | solution.py:213
  4.3 1.2 %collective-permute-start.7 = (bf16[2,192,128]{2,1,0:T(8,128)(2,1)}, bf16[2,192,128]{2,1,0:T(8,128)(2,1)S(1)}, u32[]{:S(2)}, u32[]{:S(2)}) collective-permute-start(bf16[2,192,128]{2,1,0:T(8,128)(2,1)} %block_ref.1), channel_id=1, source_target_pairs={{0,2},{1,3},{2,0},{3,1},{4,6},{5,7},{6,4},{7,5},{8,10},{9,11},{10,... | collective-permute-start | bytes 294920 | tf_op jit(solution)/shard_map/ppermute | solution.py:213
  5.5 0.0 copy-start
  5.5 0.0 collective-permute-done.refs_0_
  5.5 2.3 %collective-permute-start.8 = (bf16[2,192,128]{2,1,0:T(8,128)(2,1)}, bf16[2,192,128]{2,1,0:T(8,128)(2,1)S(1)}, u32[]{:S(2)}, u32[]{:S(2)}) collective-permute-start(bf16[2,192,128]{2,1,0:T(8,128)(2,1)} %block_ref.1), channel_id=1, source_target_pairs={{0,16},{1,17},{2,18},{3,19},{4,20},{5,21},{6,22},{7,23},{8,24},{9,... | collective-permute-start | bytes 294920 | tf_op jit(solution)/shard_map/ppermute | solution.py:213
  7.9 0.0 collective-permute-done.1.refs_1_.refs_2_
  7.9 0.0 collective-permute-done.2.refs_2_
  7.9 0.0 copy-done
  7.9 0.0 copy-start.1
  7.9 2.0 %collective-permute-start.4 = (bf16[2,192,128]{2,1,0:T(8,128)(2,1)S(1)}, bf16[2,192,128]{2,1,0:T(8,128)(2,1)S(1)}, u32[]{:S(2)}, u32[]{:S(2)}) collective-permute-start(bf16[2,192,128]{2,1,0:T(8,128)(2,1)S(1)} %shard_map.28.after_ref), channel_id=1, source_target_pairs={{0,1},{1,0},{2,3},{3,2},{4,5},{5,4},{6,7},{7,6},{8,14},{9,8},{10,1... | collective-permute-start | bytes 294920 | tf_op jit(solution)/shard_map/ppermute | solution.py:216
  9.9 0.1 collective-permute-start.5
  10.0 0.0 collective-permute-done.3.refs_3_
  10.0 0.0 collective-permute-done.7.refs_1_
  10.0 0.5 %collective-permute-start.6 = (bf16[2,192,128]{2,1,0:T(8,128)(2,1)S(1)}, bf16[2,192,128]{2,1,0:T(8,128)(2,1)S(1)}, u32[]{:S(2)}, u32[]{:S(2)}) collective-permute-start(bf16[2,192,128]{2,1,0:T(8,128)(2,1)S(1)} %get-tuple-element.28), channel_id=1, source_target_pairs={{0,1},{1,0},{2,3},{3,2},{4,6},{5,4},{6,7},{7,5},{8,10},{9,8},{10,1... | collective-permute-start | bytes 294920 | tf_op jit(solution)/shard_map/ppermute | solution.py:216
  10.5 0.0 copy-done.1
  10.5 1.4 %shard_map.30 = (f32[1,1536]{1,0:T(1,128)S(1)}, f32[1,1536]{1,0:T(1,128)S(1)}, f32[128,1536]{1,0:T(8,128)S(1)}, bf16[1536,128]{1,0:T(8,128)(2,1)S(1)}) custom-call(bf16[192,1024]{1,0:T(8,128)(2,1)S(1)} %copy-done.1, bf16[2,192,128]{2,1,0:T(8,128)(2,1)S(1)} %shard_map.29.refs_1_, bf16[2,192,128]{2,1,0:T(8,128)(2,1)S(1)} %collective-permute-done.1.refs_1_.refs_2_, ...), custom_call_target="tpu_custom_call" | custom-call | flops 4529848320 | tf_op jit(solution)/shard_map/pallas_call | solution.py:155
  11.9 0.8 %shard_map.31 = (f32[1,1536]{1,0:T(1,128)S(1)}, f32[1,1536]{1,0:T(1,128)S(1)}, f32[128,1536]{1,0:T(8,128)S(1)}, bf16[2,192,128]{2,1,0:T(8,128)(2,1)S(1)}) custom-call(bf16[1536,128]{1,0:T(8,128)(2,1)S(1)} %get-tuple-element.16.refs_0_, bf16[2,192,128]{2,1,0:T(8,128)(2,1)S(1)} %collective-permute-done.7.refs_1_, f32[1,1536]{1,0:T(1,128)S(1)} %get-tuple-element.17.refs_2_, ...), custom_call_target="tpu_custom_call" | custom-call | flops 1509949440 | tf_op jit(solution)/shard_map/pallas_call | solution.py:155
  12.7 0.7 %collective-permute-done.8.after_ref.refs_1_ = bf16[2,192,128]{2,1,0:T(8,128)(2,1)S(1)} collective-permute-done((bf16[2,192,128]{2,1,0:T(8,128)(2,1)}, bf16[2,192,128]{2,1,0:T(8,128)(2,1)S(1)}, u32[]{:S(2)}, u32[]{:S(2)}) %collective-permute-start.8) | collective-permute-done | bytes 98336 | tf_op jit(solution)/shard_map/ppermute | solution.py:213
  13.4 0.0 collective-permute-done.6
  13.4 0.0 collective-permute-done.4
  13.4 0.0 collective-permute-done.5
  13.5 0.7 %collective-permute-start.9 = (bf16[2,192,128]{2,1,0:T(8,128)(2,1)S(1)}, bf16[2,192,128]{2,1,0:T(8,128)(2,1)S(1)}, u32[]{:S(2)}, u32[]{:S(2)}) collective-permute-start(bf16[2,192,128]{2,1,0:T(8,128)(2,1)S(1)} %get-tuple-element.30), channel_id=1, source_target_pairs={{0,1},{1,0},{2,3},{3,2},{4,5},{5,4},{6,7},{7,6},{8,9},{9,8},{10,11... | collective-permute-start | bytes 294920 | tf_op jit(solution)/shard_map/ppermute | solution.py:213
  14.1 1.2 %shard_map.33 = (f32[1,1536]{1,0:T(1,128)S(1)}, f32[1,1536]{1,0:T(1,128)S(1)}, f32[128,1536]{1,0:T(8,128)S(1)}) custom-call(bf16[1536,128]{1,0:T(8,128)(2,1)S(1)} %get-tuple-element.16.refs_0_, bf16[2,192,128]{2,1,0:T(8,128)(2,1)S(1)} %collective-permute-done.8.after_ref.refs_1_, bf16[2,192,128]{2,1,0:T(8,128)(2,1)S(1)} %get-tuple-element.29.refs_2_, ...), custom_call_target="tpu_custom_call" | custom-call | flops 3019898880 | tf_op jit(solution)/shard_map/pallas_call | solution.py:155
  15.4 0.0 collective-permute-done.9
  15.4 1.5 %shard_map.34 = bf16[192,1024]{1,0:T(8,128)(2,1)} custom-call(bf16[1536,128]{1,0:T(8,128)(2,1)S(1)} %get-tuple-element.16.refs_0_, bf16[2,192,128]{2,1,0:T(8,128)(2,1)S(1)} %broadcast_select_fusion.1.refs_1_, f32[1,1536]{1,0:T(1,128)S(1)} %get-tuple-element.24.refs_2_, f32[1,1536]{1,0:T(1,128)S(1)} %get-tuple-element.25.refs_3_, ...), custom_call_target="tpu_custom_call" | custom-call | flops 1509949440 | tf_op jit(solution)/shard_map/pallas_call | solution.py:155
  (6 shorter events, 0.1 us)
Async XLA Ops:
  0.0 5.5 %collective-permute-start = (bf16[2,192,128]{2,1,0:T(8,128)(2,1)}, bf16[2,192,128]{2,1,0:T(8,128)(2,1)S(1)}, u32[]{:S(2)}, u32[]{:S(2)}) collective-permute-start(bf16[2,192,128]{2,1,0:T(8,128)(2,1)} %block_ref.1), channel_id=1, source_target_pairs={{0,16},{1,0},{2,3},{3,2},{4,1},{5,4},{6,7},{7,6},{8,9},{9,8},{10,1... | collective-permute-start | bytes 294920 | tf_op jit(solution)/shard_map/ppermute | solution.py:216
  0.1 7.8 %collective-permute-start.1 = (bf16[2,192,128]{2,1,0:T(8,128)(2,1)}, bf16[2,192,128]{2,1,0:T(8,128)(2,1)S(1)}, u32[]{:S(2)}, u32[]{:S(2)}) collective-permute-start(bf16[2,192,128]{2,1,0:T(8,128)(2,1)} %block_ref.1), channel_id=1, source_target_pairs={{0,8},{1,9},{2,10},{3,11},{4,12},{5,13},{6,14},{7,15},{8,0},{9,1},... | collective-permute-start | bytes 294920 | tf_op jit(solution)/shard_map/ppermute | solution.py:213
  2.8 5.1 %collective-permute-start.2 = (bf16[2,192,128]{2,1,0:T(8,128)(2,1)}, bf16[2,192,128]{2,1,0:T(8,128)(2,1)S(1)}, u32[]{:S(2)}, u32[]{:S(2)}) collective-permute-start(bf16[2,192,128]{2,1,0:T(8,128)(2,1)} %block_ref.1), channel_id=1, source_target_pairs={{0,24},{1,0},{2,1},{3,2},{4,5},{5,4},{6,7},{7,6},{8,9},{9,8},{10,1... | collective-permute-start | bytes 294920 | tf_op jit(solution)/shard_map/ppermute | solution.py:216
  4.1 5.9 %collective-permute-start.3 = (bf16[2,192,128]{2,1,0:T(8,128)(2,1)}, bf16[2,192,128]{2,1,0:T(8,128)(2,1)S(1)}, u32[]{:S(2)}, u32[]{:S(2)}) collective-permute-start(bf16[2,192,128]{2,1,0:T(8,128)(2,1)} %block_ref.1), channel_id=1, source_target_pairs={{0,4},{1,5},{2,6},{3,7},{4,0},{5,1},{6,2},{7,3},{8,12},{9,13},{10,... | collective-permute-start | bytes 294920 | tf_op jit(solution)/shard_map/ppermute | solution.py:213
  4.3 5.7 %collective-permute-start.7 = (bf16[2,192,128]{2,1,0:T(8,128)(2,1)}, bf16[2,192,128]{2,1,0:T(8,128)(2,1)S(1)}, u32[]{:S(2)}, u32[]{:S(2)}) collective-permute-start(bf16[2,192,128]{2,1,0:T(8,128)(2,1)} %block_ref.1), channel_id=1, source_target_pairs={{0,2},{1,3},{2,0},{3,1},{4,6},{5,7},{6,4},{7,5},{8,10},{9,11},{10,... | collective-permute-start | bytes 294920 | tf_op jit(solution)/shard_map/ppermute | solution.py:213
  5.5 2.3 %copy-start = (bf16[2,192,128]{2,1,0:T(8,128)(2,1)S(1)}, bf16[2,192,128]{2,1,0:T(8,128)(2,1)}, u32[]{:S(2)}) copy-start(bf16[2,192,128]{2,1,0:T(8,128)(2,1)} %block_ref.1) | copy-start | bytes 294916
  5.5 7.8 %collective-permute-start.8 = (bf16[2,192,128]{2,1,0:T(8,128)(2,1)}, bf16[2,192,128]{2,1,0:T(8,128)(2,1)S(1)}, u32[]{:S(2)}, u32[]{:S(2)}) collective-permute-start(bf16[2,192,128]{2,1,0:T(8,128)(2,1)} %block_ref.1), channel_id=1, source_target_pairs={{0,16},{1,17},{2,18},{3,19},{4,20},{5,21},{6,22},{7,23},{8,24},{9,... | collective-permute-start | bytes 294920 | tf_op jit(solution)/shard_map/ppermute | solution.py:213
  7.9 2.7 %copy-start.1 = (bf16[192,1024]{1,0:T(8,128)(2,1)S(1)}, bf16[192,1024]{1,0:T(8,128)(2,1)}, u32[]{:S(2)}) copy-start(bf16[192,1024]{1,0:T(8,128)(2,1)} %refs_0_.1) | copy-start | bytes 1179652
  7.9 5.5 %collective-permute-start.4 = (bf16[2,192,128]{2,1,0:T(8,128)(2,1)S(1)}, bf16[2,192,128]{2,1,0:T(8,128)(2,1)S(1)}, u32[]{:S(2)}, u32[]{:S(2)}) collective-permute-start(bf16[2,192,128]{2,1,0:T(8,128)(2,1)S(1)} %shard_map.28.after_ref), channel_id=1, source_target_pairs={{0,1},{1,0},{2,3},{3,2},{4,5},{5,4},{6,7},{7,6},{8,14},{9,8},{10,1... | collective-permute-start | bytes 294920 | tf_op jit(solution)/shard_map/ppermute | solution.py:216
  9.9 3.5 %collective-permute-start.5 = (bf16[2,192,128]{2,1,0:T(8,128)(2,1)S(1)}, bf16[2,192,128]{2,1,0:T(8,128)(2,1)S(1)}, u32[]{:S(2)}, u32[]{:S(2)}) collective-permute-start(bf16[2,192,128]{2,1,0:T(8,128)(2,1)S(1)} %shard_map.28.after_ref), channel_id=1, source_target_pairs={{0,1},{1,0},{2,3},{3,2},{4,5},{5,4},{6,7},{7,6},{8,12},{9,8},{10,1... | collective-permute-start | bytes 294920 | tf_op jit(solution)/shard_map/ppermute | solution.py:216
  10.0 3.4 %collective-permute-start.6 = (bf16[2,192,128]{2,1,0:T(8,128)(2,1)S(1)}, bf16[2,192,128]{2,1,0:T(8,128)(2,1)S(1)}, u32[]{:S(2)}, u32[]{:S(2)}) collective-permute-start(bf16[2,192,128]{2,1,0:T(8,128)(2,1)S(1)} %get-tuple-element.28), channel_id=1, source_target_pairs={{0,1},{1,0},{2,3},{3,2},{4,6},{5,4},{6,7},{7,5},{8,10},{9,8},{10,1... | collective-permute-start | bytes 294920 | tf_op jit(solution)/shard_map/ppermute | solution.py:216
  13.5 1.9 %collective-permute-start.9 = (bf16[2,192,128]{2,1,0:T(8,128)(2,1)S(1)}, bf16[2,192,128]{2,1,0:T(8,128)(2,1)S(1)}, u32[]{:S(2)}, u32[]{:S(2)}) collective-permute-start(bf16[2,192,128]{2,1,0:T(8,128)(2,1)S(1)} %get-tuple-element.30), channel_id=1, source_target_pairs={{0,1},{1,0},{2,3},{3,2},{4,5},{5,4},{6,7},{7,6},{8,9},{9,8},{10,11... | collective-permute-start | bytes 294920 | tf_op jit(solution)/shard_map/ppermute | solution.py:213

commit v7 on v6

--- a/solution.py
+++ b/solution.py
@@ -228,7 +228,7 @@
             for holder, got in (later | {0: own}).items():
                 filled = jnp.where(me == holder, got, filled)
         came = [(send(filled, wave[-1]), [t for _, t in wave[-1]])]
-        came += [(send(first, real), [t for _, t in real]) for real in wave[-2::-1]]
+        came += [(send(first, real), [t for _, t in real]) for real in wave[:-1]]
         first = filled
         if k == 0:
             for bit in range(1, levels - 2):

time: 17.1 us -> 17.1 us (level)
  no operation moved by 1% of the time
where the time goes in v7:
time: 17.1 us; the launch traced here: 16.9 us
  starting transfers between devices  11.1 us (65%)
  Pallas kernels  4.97 us (29%)
  waiting for transfers between devices  0.67 us (4%)
    ppermute x5, starting transfers between devices, swap(): return lax.ppermute(value, AXIS, [(i, i ^ 1 << bit) for i in range(count)])  7.14 us
    pallas_call x4, Pallas kernels, attend(): pl.pallas_call(functools.partial(attend_body, len(blocks), state is None,...  4.95 us
    ppermute x5, starting transfers between devices, send(): return lax.ppermute(value, AXIS, fill(real, count))  3.94 us
    ppermute x5, waiting for transfers between devices, swap(): return lax.ppermute(value, AXIS, [(i, i ^ 1 << bit) for i in range(count)])  0.65 us
  transfers between devices with their start and end apart: 10, of which 1 were waited for; matrix products, arithmetic and copies ran while one was open for 0% of the time, Pallas kernels for 21%

profile of v7, /device:TPU:1, one launch (start us, length us, event | category | flops | bytes accessed | tf_op | source)
XLA Modules:
  0.0 16.9 jit_solution(13563623183063441807)
XLA Ops:
  0.0 0.1 collective-permute-start
  0.1 2.7 %collective-permute-start.1 = (bf16[2,192,128]{2,1,0:T(8,128)(2,1)}, bf16[2,192,128]{2,1,0:T(8,128)(2,1)S(1)}, u32[]{:S(2)}, u32[]{:S(2)}) collective-permute-start(bf16[2,192,128]{2,1,0:T(8,128)(2,1)} %block_ref.1), channel_id=1, source_target_pairs={{0,8},{1,9},{2,10},{3,11},{4,12},{5,13},{6,14},{7,15},{8,0},{9,1},... | collective-permute-start | bytes 294920 | tf_op jit(solution)/shard_map/ppermute | solution.py:213
  2.8 1.3 %collective-permute-start.2 = (bf16[2,192,128]{2,1,0:T(8,128)(2,1)}, bf16[2,192,128]{2,1,0:T(8,128)(2,1)S(1)}, u32[]{:S(2)}, u32[]{:S(2)}) collective-permute-start(bf16[2,192,128]{2,1,0:T(8,128)(2,1)} %block_ref.1), channel_id=1, source_target_pairs={{0,24},{1,0},{2,1},{3,2},{4,5},{5,4},{6,7},{7,6},{8,9},{9,8},{10,1... | collective-permute-start | bytes 294920 | tf_op jit(solution)/shard_map/ppermute | solution.py:216
  4.1 0.2 %collective-permute-start.3 = (bf16[2,192,128]{2,1,0:T(8,128)(2,1)}, bf16[2,192,128]{2,1,0:T(8,128)(2,1)S(1)}, u32[]{:S(2)}, u32[]{:S(2)}) collective-permute-start(bf16[2,192,128]{2,1,0:T(8,128)(2,1)} %block_ref.1), channel_id=1, source_target_pairs={{0,4},{1,5},{2,6},{3,7},{4,0},{5,1},{6,2},{7,3},{8,12},{9,13},{10,... | collective-permute-start | bytes 294920 | tf_op jit(solution)/shard_map/ppermute | solution.py:213
  4.3 1.2 %collective-permute-start.7 = (bf16[2,192,128]{2,1,0:T(8,128)(2,1)}, bf16[2,192,128]{2,1,0:T(8,128)(2,1)S(1)}, u32[]{:S(2)}, u32[]{:S(2)}) collective-permute-start(bf16[2,192,128]{2,1,0:T(8,128)(2,1)} %block_ref.1), channel_id=1, source_target_pairs={{0,2},{1,3},{2,0},{3,1},{4,6},{5,7},{6,4},{7,5},{8,10},{9,11},{10,... | collective-permute-start | bytes 294920 | tf_op jit(solution)/shard_map/ppermute | solution.py:213
  5.5 0.0 copy-start
  5.5 0.0 collective-permute-done.refs_0_
  5.5 2.3 %collective-permute-start.8 = (bf16[2,192,128]{2,1,0:T(8,128)(2,1)}, bf16[2,192,128]{2,1,0:T(8,128)(2,1)S(1)}, u32[]{:S(2)}, u32[]{:S(2)}) collective-permute-start(bf16[2,192,128]{2,1,0:T(8,128)(2,1)} %block_ref.1), channel_id=1, source_target_pairs={{0,16},{1,17},{2,18},{3,19},{4,20},{5,21},{6,22},{7,23},{8,24},{9,... | collective-permute-start | bytes 294920 | tf_op jit(solution)/shard_map/ppermute | solution.py:213
  7.9 0.0 collective-permute-done.1.refs_1_.refs_2_
  7.9 0.0 collective-permute-done.2.refs_2_
  7.9 0.0 copy-done
  7.9 0.0 copy-start.1
  7.9 2.0 %collective-permute-start.4 = (bf16[2,192,128]{2,1,0:T(8,128)(2,1)S(1)}, bf16[2,192,128]{2,1,0:T(8,128)(2,1)S(1)}, u32[]{:S(2)}, u32[]{:S(2)}) collective-permute-start(bf16[2,192,128]{2,1,0:T(8,128)(2,1)S(1)} %shard_map.28.after_ref), channel_id=1, source_target_pairs={{0,1},{1,0},{2,3},{3,2},{4,5},{5,4},{6,7},{7,6},{8,12},{9,8},{10,1... | collective-permute-start | bytes 294920 | tf_op jit(solution)/shard_map/ppermute | solution.py:216
  9.9 0.1 collective-permute-start.5
  10.0 0.0 collective-permute-done.3.refs_3_
  10.0 0.0 collective-permute-done.7.refs_1_
  10.0 0.5 %collective-permute-start.6 = (bf16[2,192,128]{2,1,0:T(8,128)(2,1)S(1)}, bf16[2,192,128]{2,1,0:T(8,128)(2,1)S(1)}, u32[]{:S(2)}, u32[]{:S(2)}) collective-permute-start(bf16[2,192,128]{2,1,0:T(8,128)(2,1)S(1)} %get-tuple-element.28), channel_id=1, source_target_pairs={{0,1},{1,0},{2,3},{3,2},{4,6},{5,4},{6,7},{7,5},{8,10},{9,8},{10,1... | collective-permute-start | bytes 294920 | tf_op jit(solution)/shard_map/ppermute | solution.py:216
  10.5 0.0 copy-done.1
  10.5 1.4 %shard_map.30 = (f32[1,1536]{1,0:T(1,128)S(1)}, f32[1,1536]{1,0:T(1,128)S(1)}, f32[128,1536]{1,0:T(8,128)S(1)}, bf16[1536,128]{1,0:T(8,128)(2,1)S(1)}) custom-call(bf16[192,1024]{1,0:T(8,128)(2,1)S(1)} %copy-done.1, bf16[2,192,128]{2,1,0:T(8,128)(2,1)S(1)} %shard_map.29.refs_1_, bf16[2,192,128]{2,1,0:T(8,128)(2,1)S(1)} %collective-permute-done.1.refs_1_.refs_2_, ...), custom_call_target="tpu_custom_call" | custom-call | flops 4529848320 | tf_op jit(solution)/shard_map/pallas_call | solution.py:155
  11.9 0.8 %shard_map.31 = (f32[1,1536]{1,0:T(1,128)S(1)}, f32[1,1536]{1,0:T(1,128)S(1)}, f32[128,1536]{1,0:T(8,128)S(1)}, bf16[2,192,128]{2,1,0:T(8,128)(2,1)S(1)}) custom-call(bf16[1536,128]{1,0:T(8,128)(2,1)S(1)} %get-tuple-element.16.refs_0_, bf16[2,192,128]{2,1,0:T(8,128)(2,1)S(1)} %collective-permute-done.7.refs_1_, f32[1,1536]{1,0:T(1,128)S(1)} %get-tuple-element.17.refs_2_, ...), custom_call_target="tpu_custom_call" | custom-call | flops 1509949440 | tf_op jit(solution)/shard_map/pallas_call | solution.py:155
  12.7 0.6 %collective-permute-done.8.after_ref.refs_1_ = bf16[2,192,128]{2,1,0:T(8,128)(2,1)S(1)} collective-permute-done((bf16[2,192,128]{2,1,0:T(8,128)(2,1)}, bf16[2,192,128]{2,1,0:T(8,128)(2,1)S(1)}, u32[]{:S(2)}, u32[]{:S(2)}) %collective-permute-start.8) | collective-permute-done | bytes 98336 | tf_op jit(solution)/shard_map/ppermute | solution.py:213
  13.4 0.0 collective-permute-done.6
  13.4 0.0 collective-permute-done.4
  13.4 0.0 collective-permute-done.5
  13.5 0.7 %collective-permute-start.9 = (bf16[2,192,128]{2,1,0:T(8,128)(2,1)S(1)}, bf16[2,192,128]{2,1,0:T(8,128)(2,1)S(1)}, u32[]{:S(2)}, u32[]{:S(2)}) collective-permute-start(bf16[2,192,128]{2,1,0:T(8,128)(2,1)S(1)} %get-tuple-element.30), channel_id=1, source_target_pairs={{0,1},{1,0},{2,3},{3,2},{4,5},{5,4},{6,7},{7,6},{8,9},{9,8},{10,11... | collective-permute-start | bytes 294920 | tf_op jit(solution)/shard_map/ppermute | solution.py:213
  14.1 1.2 %shard_map.33 = (f32[1,1536]{1,0:T(1,128)S(1)}, f32[1,1536]{1,0:T(1,128)S(1)}, f32[128,1536]{1,0:T(8,128)S(1)}) custom-call(bf16[1536,128]{1,0:T(8,128)(2,1)S(1)} %get-tuple-element.16.refs_0_, bf16[2,192,128]{2,1,0:T(8,128)(2,1)S(1)} %collective-permute-done.8.after_ref.refs_1_, bf16[2,192,128]{2,1,0:T(8,128)(2,1)S(1)} %get-tuple-element.29.refs_2_, ...), custom_call_target="tpu_custom_call" | custom-call | flops 3019898880 | tf_op jit(solution)/shard_map/pallas_call | solution.py:155
  15.4 0.0 collective-permute-done.9
  15.4 1.5 %shard_map.34 = bf16[192,1024]{1,0:T(8,128)(2,1)} custom-call(bf16[1536,128]{1,0:T(8,128)(2,1)S(1)} %get-tuple-element.16.refs_0_, bf16[2,192,128]{2,1,0:T(8,128)(2,1)S(1)} %broadcast_select_fusion.1.refs_1_, f32[1,1536]{1,0:T(1,128)S(1)} %get-tuple-element.24.refs_2_, f32[1,1536]{1,0:T(1,128)S(1)} %get-tuple-element.25.refs_3_, ...), custom_call_target="tpu_custom_call" | custom-call | flops 1509949440 | tf_op jit(solution)/shard_map/pallas_call | solution.py:155
  (6 shorter events, 0.1 us)
Async XLA Ops:
  0.0 5.5 %collective-permute-start = (bf16[2,192,128]{2,1,0:T(8,128)(2,1)}, bf16[2,192,128]{2,1,0:T(8,128)(2,1)S(1)}, u32[]{:S(2)}, u32[]{:S(2)}) collective-permute-start(bf16[2,192,128]{2,1,0:T(8,128)(2,1)} %block_ref.1), channel_id=1, source_target_pairs={{0,16},{1,0},{2,3},{3,2},{4,1},{5,4},{6,7},{7,6},{8,9},{9,8},{10,1... | collective-permute-start | bytes 294920 | tf_op jit(solution)/shard_map/ppermute | solution.py:216
  0.1 7.8 %collective-permute-start.1 = (bf16[2,192,128]{2,1,0:T(8,128)(2,1)}, bf16[2,192,128]{2,1,0:T(8,128)(2,1)S(1)}, u32[]{:S(2)}, u32[]{:S(2)}) collective-permute-start(bf16[2,192,128]{2,1,0:T(8,128)(2,1)} %block_ref.1), channel_id=1, source_target_pairs={{0,8},{1,9},{2,10},{3,11},{4,12},{5,13},{6,14},{7,15},{8,0},{9,1},... | collective-permute-start | bytes 294920 | tf_op jit(solution)/shard_map/ppermute | solution.py:213
  2.8 5.1 %collective-permute-start.2 = (bf16[2,192,128]{2,1,0:T(8,128)(2,1)}, bf16[2,192,128]{2,1,0:T(8,128)(2,1)S(1)}, u32[]{:S(2)}, u32[]{:S(2)}) collective-permute-start(bf16[2,192,128]{2,1,0:T(8,128)(2,1)} %block_ref.1), channel_id=1, source_target_pairs={{0,24},{1,0},{2,1},{3,2},{4,5},{5,4},{6,7},{7,6},{8,9},{9,8},{10,1... | collective-permute-start | bytes 294920 | tf_op jit(solution)/shard_map/ppermute | solution.py:216
  4.1 5.9 %collective-permute-start.3 = (bf16[2,192,128]{2,1,0:T(8,128)(2,1)}, bf16[2,192,128]{2,1,0:T(8,128)(2,1)S(1)}, u32[]{:S(2)}, u32[]{:S(2)}) collective-permute-start(bf16[2,192,128]{2,1,0:T(8,128)(2,1)} %block_ref.1), channel_id=1, source_target_pairs={{0,4},{1,5},{2,6},{3,7},{4,0},{5,1},{6,2},{7,3},{8,12},{9,13},{10,... | collective-permute-start | bytes 294920 | tf_op jit(solution)/shard_map/ppermute | solution.py:213
  4.3 5.7 %collective-permute-start.7 = (bf16[2,192,128]{2,1,0:T(8,128)(2,1)}, bf16[2,192,128]{2,1,0:T(8,128)(2,1)S(1)}, u32[]{:S(2)}, u32[]{:S(2)}) collective-permute-start(bf16[2,192,128]{2,1,0:T(8,128)(2,1)} %block_ref.1), channel_id=1, source_target_pairs={{0,2},{1,3},{2,0},{3,1},{4,6},{5,7},{6,4},{7,5},{8,10},{9,11},{10,... | collective-permute-start | bytes 294920 | tf_op jit(solution)/shard_map/ppermute | solution.py:213
  5.5 2.3 %copy-start = (bf16[2,192,128]{2,1,0:T(8,128)(2,1)S(1)}, bf16[2,192,128]{2,1,0:T(8,128)(2,1)}, u32[]{:S(2)}) copy-start(bf16[2,192,128]{2,1,0:T(8,128)(2,1)} %block_ref.1) | copy-start | bytes 294916
  5.5 7.8 %collective-permute-start.8 = (bf16[2,192,128]{2,1,0:T(8,128)(2,1)}, bf16[2,192,128]{2,1,0:T(8,128)(2,1)S(1)}, u32[]{:S(2)}, u32[]{:S(2)}) collective-permute-start(bf16[2,192,128]{2,1,0:T(8,128)(2,1)} %block_ref.1), channel_id=1, source_target_pairs={{0,16},{1,17},{2,18},{3,19},{4,20},{5,21},{6,22},{7,23},{8,24},{9,... | collective-permute-start | bytes 294920 | tf_op jit(solution)/shard_map/ppermute | solution.py:213
  7.9 2.7 %copy-start.1 = (bf16[192,1024]{1,0:T(8,128)(2,1)S(1)}, bf16[192,1024]{1,0:T(8,128)(2,1)}, u32[]{:S(2)}) copy-start(bf16[192,1024]{1,0:T(8,128)(2,1)} %refs_0_.1) | copy-start | bytes 1179652
  7.9 5.5 %collective-permute-start.4 = (bf16[2,192,128]{2,1,0:T(8,128)(2,1)S(1)}, bf16[2,192,128]{2,1,0:T(8,128)(2,1)S(1)}, u32[]{:S(2)}, u32[]{:S(2)}) collective-permute-start(bf16[2,192,128]{2,1,0:T(8,128)(2,1)S(1)} %shard_map.28.after_ref), channel_id=1, source_target_pairs={{0,1},{1,0},{2,3},{3,2},{4,5},{5,4},{6,7},{7,6},{8,12},{9,8},{10,1... | collective-permute-start | bytes 294920 | tf_op jit(solution)/shard_map/ppermute | solution.py:216
  9.9 3.5 %collective-permute-start.5 = (bf16[2,192,128]{2,1,0:T(8,128)(2,1)S(1)}, bf16[2,192,128]{2,1,0:T(8,128)(2,1)S(1)}, u32[]{:S(2)}, u32[]{:S(2)}) collective-permute-start(bf16[2,192,128]{2,1,0:T(8,128)(2,1)S(1)} %shard_map.28.after_ref), channel_id=1, source_target_pairs={{0,1},{1,0},{2,3},{3,2},{4,5},{5,4},{6,7},{7,6},{8,14},{9,8},{10,1... | collective-permute-start | bytes 294920 | tf_op jit(solution)/shard_map/ppermute | solution.py:216
  10.0 3.4 %collective-permute-start.6 = (bf16[2,192,128]{2,1,0:T(8,128)(2,1)S(1)}, bf16[2,192,128]{2,1,0:T(8,128)(2,1)S(1)}, u32[]{:S(2)}, u32[]{:S(2)}) collective-permute-start(bf16[2,192,128]{2,1,0:T(8,128)(2,1)S(1)} %get-tuple-element.28), channel_id=1, source_target_pairs={{0,1},{1,0},{2,3},{3,2},{4,6},{5,4},{6,7},{7,5},{8,10},{9,8},{10,1... | collective-permute-start | bytes 294920 | tf_op jit(solution)/shard_map/ppermute | solution.py:216
  13.5 1.9 %collective-permute-start.9 = (bf16[2,192,128]{2,1,0:T(8,128)(2,1)S(1)}, bf16[2,192,128]{2,1,0:T(8,128)(2,1)S(1)}, u32[]{:S(2)}, u32[]{:S(2)}) collective-permute-start(bf16[2,192,128]{2,1,0:T(8,128)(2,1)S(1)} %get-tuple-element.30), channel_id=1, source_target_pairs={{0,1},{1,0},{2,3},{3,2},{4,5},{5,4},{6,7},{7,6},{8,9},{9,8},{10,11... | collective-permute-start | bytes 294920 | tf_op jit(solution)/shard_map/ppermute | solution.py:213

commit v8 on v7

--- a/solution.py
+++ b/solution.py
@@ -11,7 +11,7 @@
 HD = 128
 AXIS = "seq"
 FANOUT = 3
-CHUNK = 512
+CHUNK = 768
 LAST_CHUNK = 768
 LOG2E = math.log2(math.e)
 VMEM = pl.BlockSpec(memory_space=pltpu.VMEM)

time: 17.1 us -> 17.1 us (level)
  transfers between devices with their start and end apart: 10 -> 10, of which waited for: 1 -> 1; matrix products, arithmetic and copies ran while one was open for 0% -> 0% of each run, Pallas kernels for 21% -> 20%
where the time goes in v8:
time: 17.1 us; the launch traced here: 16.9 us
  starting transfers between devices  11.1 us (65%)
  Pallas kernels  4.87 us (28%)
  waiting for transfers between devices  0.78 us (5%)
    ppermute x5, starting transfers between devices, swap(): return lax.ppermute(value, AXIS, [(i, i ^ 1 << bit) for i in range(count)])  7.14 us
    pallas_call x4, Pallas kernels, attend(): pl.pallas_call(functools.partial(attend_body, len(blocks), state is None,...  4.86 us
    ppermute x5, starting transfers between devices, send(): return lax.ppermute(value, AXIS, fill(real, count))  3.94 us
    ppermute x5, waiting for transfers between devices, swap(): return lax.ppermute(value, AXIS, [(i, i ^ 1 << bit) for i in range(count)])  0.76 us
  transfers between devices with their start and end apart: 10, of which 1 were waited for; matrix products, arithmetic and copies ran while one was open for 0% of the time, Pallas kernels for 20%

profile of v8, /device:TPU:1, one launch (start us, length us, event | category | flops | bytes accessed | tf_op | source)
XLA Modules:
  0.0 16.9 jit_solution(9390454257346373974)
XLA Ops:
  0.0 0.1 collective-permute-start
  0.1 2.7 %collective-permute-start.1 = (bf16[2,192,128]{2,1,0:T(8,128)(2,1)}, bf16[2,192,128]{2,1,0:T(8,128)(2,1)S(1)}, u32[]{:S(2)}, u32[]{:S(2)}) collective-permute-start(bf16[2,192,128]{2,1,0:T(8,128)(2,1)} %block_ref.1), channel_id=1, source_target_pairs={{0,8},{1,9},{2,10},{3,11},{4,12},{5,13},{6,14},{7,15},{8,0},{9,1},... | collective-permute-start | bytes 294920 | tf_op jit(solution)/shard_map/ppermute | solution.py:213
  2.8 1.3 %collective-permute-start.2 = (bf16[2,192,128]{2,1,0:T(8,128)(2,1)}, bf16[2,192,128]{2,1,0:T(8,128)(2,1)S(1)}, u32[]{:S(2)}, u32[]{:S(2)}) collective-permute-start(bf16[2,192,128]{2,1,0:T(8,128)(2,1)} %block_ref.1), channel_id=1, source_target_pairs={{0,24},{1,0},{2,1},{3,2},{4,5},{5,4},{6,7},{7,6},{8,9},{9,8},{10,1... | collective-permute-start | bytes 294920 | tf_op jit(solution)/shard_map/ppermute | solution.py:216
  4.1 0.2 %collective-permute-start.3 = (bf16[2,192,128]{2,1,0:T(8,128)(2,1)}, bf16[2,192,128]{2,1,0:T(8,128)(2,1)S(1)}, u32[]{:S(2)}, u32[]{:S(2)}) collective-permute-start(bf16[2,192,128]{2,1,0:T(8,128)(2,1)} %block_ref.1), channel_id=1, source_target_pairs={{0,4},{1,5},{2,6},{3,7},{4,0},{5,1},{6,2},{7,3},{8,12},{9,13},{10,... | collective-permute-start | bytes 294920 | tf_op jit(solution)/shard_map/ppermute | solution.py:213
  4.3 1.2 %collective-permute-start.7 = (bf16[2,192,128]{2,1,0:T(8,128)(2,1)}, bf16[2,192,128]{2,1,0:T(8,128)(2,1)S(1)}, u32[]{:S(2)}, u32[]{:S(2)}) collective-permute-start(bf16[2,192,128]{2,1,0:T(8,128)(2,1)} %block_ref.1), channel_id=1, source_target_pairs={{0,2},{1,3},{2,0},{3,1},{4,6},{5,7},{6,4},{7,5},{8,10},{9,11},{10,... | collective-permute-start | bytes 294920 | tf_op jit(solution)/shard_map/ppermute | solution.py:213
  5.5 0.0 copy-start
  5.5 0.0 collective-permute-done.refs_0_
  5.5 2.3 %collective-permute-start.8 = (bf16[2,192,128]{2,1,0:T(8,128)(2,1)}, bf16[2,192,128]{2,1,0:T(8,128)(2,1)S(1)}, u32[]{:S(2)}, u32[]{:S(2)}) collective-permute-start(bf16[2,192,128]{2,1,0:T(8,128)(2,1)} %block_ref.1), channel_id=1, source_target_pairs={{0,16},{1,17},{2,18},{3,19},{4,20},{5,21},{6,22},{7,23},{8,24},{9,... | collective-permute-start | bytes 294920 | tf_op jit(solution)/shard_map/ppermute | solution.py:213
  7.9 0.0 collective-permute-done.1.refs_1_.refs_2_
  7.9 0.0 collective-permute-done.2.refs_2_
  7.9 0.0 copy-done
  7.9 0.0 copy-start.1
  7.9 2.0 %collective-permute-start.4 = (bf16[2,192,128]{2,1,0:T(8,128)(2,1)S(1)}, bf16[2,192,128]{2,1,0:T(8,128)(2,1)S(1)}, u32[]{:S(2)}, u32[]{:S(2)}) collective-permute-start(bf16[2,192,128]{2,1,0:T(8,128)(2,1)S(1)} %shard_map.28.after_ref), channel_id=1, source_target_pairs={{0,1},{1,0},{2,3},{3,2},{4,5},{5,4},{6,7},{7,6},{8,12},{9,8},{10,1... | collective-permute-start | bytes 294920 | tf_op jit(solution)/shard_map/ppermute | solution.py:216
  9.9 0.1 collective-permute-start.5
  10.0 0.0 collective-permute-done.3.refs_3_
  10.0 0.0 collective-permute-done.7.refs_1_
  10.0 0.5 %collective-permute-start.6 = (bf16[2,192,128]{2,1,0:T(8,128)(2,1)S(1)}, bf16[2,192,128]{2,1,0:T(8,128)(2,1)S(1)}, u32[]{:S(2)}, u32[]{:S(2)}) collective-permute-start(bf16[2,192,128]{2,1,0:T(8,128)(2,1)S(1)} %get-tuple-element.28), channel_id=1, source_target_pairs={{0,1},{1,0},{2,3},{3,2},{4,6},{5,4},{6,7},{7,5},{8,10},{9,8},{10,1... | collective-permute-start | bytes 294920 | tf_op jit(solution)/shard_map/ppermute | solution.py:216
  10.5 0.0 copy-done.1
  10.5 1.4 %shard_map.30 = (f32[1,1536]{1,0:T(1,128)S(1)}, f32[1,1536]{1,0:T(1,128)S(1)}, f32[128,1536]{1,0:T(8,128)S(1)}, bf16[1536,128]{1,0:T(8,128)(2,1)S(1)}) custom-call(bf16[192,1024]{1,0:T(8,128)(2,1)S(1)} %copy-done.1, bf16[2,192,128]{2,1,0:T(8,128)(2,1)S(1)} %shard_map.29.refs_1_, bf16[2,192,128]{2,1,0:T(8,128)(2,1)S(1)} %collective-permute-done.1.refs_1_.refs_2_, ...), custom_call_target="tpu_custom_call" | custom-call | flops 4529848320 | tf_op jit(solution)/shard_map/pallas_call | solution.py:155
  11.9 0.7 %shard_map.31 = (f32[1,1536]{1,0:T(1,128)S(1)}, f32[1,1536]{1,0:T(1,128)S(1)}, f32[128,1536]{1,0:T(8,128)S(1)}, bf16[2,192,128]{2,1,0:T(8,128)(2,1)S(1)}) custom-call(bf16[1536,128]{1,0:T(8,128)(2,1)S(1)} %get-tuple-element.16.refs_0_, bf16[2,192,128]{2,1,0:T(8,128)(2,1)S(1)} %collective-permute-done.7.refs_1_, f32[1,1536]{1,0:T(1,128)S(1)} %get-tuple-element.17.refs_2_, ...), custom_call_target="tpu_custom_call" | custom-call | flops 1509949440 | tf_op jit(solution)/shard_map/pallas_call | solution.py:155
  12.6 0.8 %collective-permute-done.8.after_ref.refs_1_ = bf16[2,192,128]{2,1,0:T(8,128)(2,1)S(1)} collective-permute-done((bf16[2,192,128]{2,1,0:T(8,128)(2,1)}, bf16[2,192,128]{2,1,0:T(8,128)(2,1)S(1)}, u32[]{:S(2)}, u32[]{:S(2)}) %collective-permute-start.8) | collective-permute-done | bytes 98336 | tf_op jit(solution)/shard_map/ppermute | solution.py:213
  13.4 0.0 collective-permute-done.6
  13.4 0.0 collective-permute-done.4
  13.4 0.0 collective-permute-done.5
  13.5 0.7 %collective-permute-start.9 = (bf16[2,192,128]{2,1,0:T(8,128)(2,1)S(1)}, bf16[2,192,128]{2,1,0:T(8,128)(2,1)S(1)}, u32[]{:S(2)}, u32[]{:S(2)}) collective-permute-start(bf16[2,192,128]{2,1,0:T(8,128)(2,1)S(1)} %get-tuple-element.30), channel_id=1, source_target_pairs={{0,1},{1,0},{2,3},{3,2},{4,5},{5,4},{6,7},{7,6},{8,9},{9,8},{10,11... | collective-permute-start | bytes 294920 | tf_op jit(solution)/shard_map/ppermute | solution.py:213
  14.1 1.3 %shard_map.33 = (f32[1,1536]{1,0:T(1,128)S(1)}, f32[1,1536]{1,0:T(1,128)S(1)}, f32[128,1536]{1,0:T(8,128)S(1)}) custom-call(bf16[1536,128]{1,0:T(8,128)(2,1)S(1)} %get-tuple-element.16.refs_0_, bf16[2,192,128]{2,1,0:T(8,128)(2,1)S(1)} %collective-permute-done.8.after_ref.refs_1_, bf16[2,192,128]{2,1,0:T(8,128)(2,1)S(1)} %get-tuple-element.29.refs_2_, ...), custom_call_target="tpu_custom_call" | custom-call | flops 3019898880 | tf_op jit(solution)/shard_map/pallas_call | solution.py:155
  15.4 0.0 collective-permute-done.9
  15.4 1.5 %shard_map.34 = bf16[192,1024]{1,0:T(8,128)(2,1)} custom-call(bf16[1536,128]{1,0:T(8,128)(2,1)S(1)} %get-tuple-element.16.refs_0_, bf16[2,192,128]{2,1,0:T(8,128)(2,1)S(1)} %broadcast_select_fusion.1.refs_1_, f32[1,1536]{1,0:T(1,128)S(1)} %get-tuple-element.24.refs_2_, f32[1,1536]{1,0:T(1,128)S(1)} %get-tuple-element.25.refs_3_, ...), custom_call_target="tpu_custom_call" | custom-call | flops 1509949440 | tf_op jit(solution)/shard_map/pallas_call | solution.py:155
  (6 shorter events, 0.1 us)
Async XLA Ops:
  0.0 5.5 %collective-permute-start = (bf16[2,192,128]{2,1,0:T(8,128)(2,1)}, bf16[2,192,128]{2,1,0:T(8,128)(2,1)S(1)}, u32[]{:S(2)}, u32[]{:S(2)}) collective-permute-start(bf16[2,192,128]{2,1,0:T(8,128)(2,1)} %block_ref.1), channel_id=1, source_target_pairs={{0,16},{1,0},{2,3},{3,2},{4,1},{5,4},{6,7},{7,6},{8,9},{9,8},{10,1... | collective-permute-start | bytes 294920 | tf_op jit(solution)/shard_map/ppermute | solution.py:216
  0.1 7.8 %collective-permute-start.1 = (bf16[2,192,128]{2,1,0:T(8,128)(2,1)}, bf16[2,192,128]{2,1,0:T(8,128)(2,1)S(1)}, u32[]{:S(2)}, u32[]{:S(2)}) collective-permute-start(bf16[2,192,128]{2,1,0:T(8,128)(2,1)} %block_ref.1), channel_id=1, source_target_pairs={{0,8},{1,9},{2,10},{3,11},{4,12},{5,13},{6,14},{7,15},{8,0},{9,1},... | collective-permute-start | bytes 294920 | tf_op jit(solution)/shard_map/ppermute | solution.py:213
  2.8 5.1 %collective-permute-start.2 = (bf16[2,192,128]{2,1,0:T(8,128)(2,1)}, bf16[2,192,128]{2,1,0:T(8,128)(2,1)S(1)}, u32[]{:S(2)}, u32[]{:S(2)}) collective-permute-start(bf16[2,192,128]{2,1,0:T(8,128)(2,1)} %block_ref.1), channel_id=1, source_target_pairs={{0,24},{1,0},{2,1},{3,2},{4,5},{5,4},{6,7},{7,6},{8,9},{9,8},{10,1... | collective-permute-start | bytes 294920 | tf_op jit(solution)/shard_map/ppermute | solution.py:216
  4.1 5.9 %collective-permute-start.3 = (bf16[2,192,128]{2,1,0:T(8,128)(2,1)}, bf16[2,192,128]{2,1,0:T(8,128)(2,1)S(1)}, u32[]{:S(2)}, u32[]{:S(2)}) collective-permute-start(bf16[2,192,128]{2,1,0:T(8,128)(2,1)} %block_ref.1), channel_id=1, source_target_pairs={{0,4},{1,5},{2,6},{3,7},{4,0},{5,1},{6,2},{7,3},{8,12},{9,13},{10,... | collective-permute-start | bytes 294920 | tf_op jit(solution)/shard_map/ppermute | solution.py:213
  4.3 5.7 %collective-permute-start.7 = (bf16[2,192,128]{2,1,0:T(8,128)(2,1)}, bf16[2,192,128]{2,1,0:T(8,128)(2,1)S(1)}, u32[]{:S(2)}, u32[]{:S(2)}) collective-permute-start(bf16[2,192,128]{2,1,0:T(8,128)(2,1)} %block_ref.1), channel_id=1, source_target_pairs={{0,2},{1,3},{2,0},{3,1},{4,6},{5,7},{6,4},{7,5},{8,10},{9,11},{10,... | collective-permute-start | bytes 294920 | tf_op jit(solution)/shard_map/ppermute | solution.py:213
  5.5 2.3 %copy-start = (bf16[2,192,128]{2,1,0:T(8,128)(2,1)S(1)}, bf16[2,192,128]{2,1,0:T(8,128)(2,1)}, u32[]{:S(2)}) copy-start(bf16[2,192,128]{2,1,0:T(8,128)(2,1)} %block_ref.1) | copy-start | bytes 294916
  5.5 7.8 %collective-permute-start.8 = (bf16[2,192,128]{2,1,0:T(8,128)(2,1)}, bf16[2,192,128]{2,1,0:T(8,128)(2,1)S(1)}, u32[]{:S(2)}, u32[]{:S(2)}) collective-permute-start(bf16[2,192,128]{2,1,0:T(8,128)(2,1)} %block_ref.1), channel_id=1, source_target_pairs={{0,16},{1,17},{2,18},{3,19},{4,20},{5,21},{6,22},{7,23},{8,24},{9,... | collective-permute-start | bytes 294920 | tf_op jit(solution)/shard_map/ppermute | solution.py:213
  7.9 2.7 %copy-start.1 = (bf16[192,1024]{1,0:T(8,128)(2,1)S(1)}, bf16[192,1024]{1,0:T(8,128)(2,1)}, u32[]{:S(2)}) copy-start(bf16[192,1024]{1,0:T(8,128)(2,1)} %refs_0_.1) | copy-start | bytes 1179652
  7.9 5.5 %collective-permute-start.4 = (bf16[2,192,128]{2,1,0:T(8,128)(2,1)S(1)}, bf16[2,192,128]{2,1,0:T(8,128)(2,1)S(1)}, u32[]{:S(2)}, u32[]{:S(2)}) collective-permute-start(bf16[2,192,128]{2,1,0:T(8,128)(2,1)S(1)} %shard_map.28.after_ref), channel_id=1, source_target_pairs={{0,1},{1,0},{2,3},{3,2},{4,5},{5,4},{6,7},{7,6},{8,12},{9,8},{10,1... | collective-permute-start | bytes 294920 | tf_op jit(solution)/shard_map/ppermute | solution.py:216
  9.9 3.5 %collective-permute-start.5 = (bf16[2,192,128]{2,1,0:T(8,128)(2,1)S(1)}, bf16[2,192,128]{2,1,0:T(8,128)(2,1)S(1)}, u32[]{:S(2)}, u32[]{:S(2)}) collective-permute-start(bf16[2,192,128]{2,1,0:T(8,128)(2,1)S(1)} %shard_map.28.after_ref), channel_id=1, source_target_pairs={{0,1},{1,0},{2,3},{3,2},{4,5},{5,4},{6,7},{7,6},{8,14},{9,8},{10,1... | collective-permute-start | bytes 294920 | tf_op jit(solution)/shard_map/ppermute | solution.py:216
  10.0 3.4 %collective-permute-start.6 = (bf16[2,192,128]{2,1,0:T(8,128)(2,1)S(1)}, bf16[2,192,128]{2,1,0:T(8,128)(2,1)S(1)}, u32[]{:S(2)}, u32[]{:S(2)}) collective-permute-start(bf16[2,192,128]{2,1,0:T(8,128)(2,1)S(1)} %get-tuple-element.28), channel_id=1, source_target_pairs={{0,1},{1,0},{2,3},{3,2},{4,6},{5,4},{6,7},{7,5},{8,10},{9,8},{10,1... | collective-permute-start | bytes 294920 | tf_op jit(solution)/shard_map/ppermute | solution.py:216
  13.5 1.9 %collective-permute-start.9 = (bf16[2,192,128]{2,1,0:T(8,128)(2,1)S(1)}, bf16[2,192,128]{2,1,0:T(8,128)(2,1)S(1)}, u32[]{:S(2)}, u32[]{:S(2)}) collective-permute-start(bf16[2,192,128]{2,1,0:T(8,128)(2,1)S(1)} %get-tuple-element.30), channel_id=1, source_target_pairs={{0,1},{1,0},{2,3},{3,2},{4,5},{5,4},{6,7},{7,6},{8,9},{9,8},{10,11... | collective-permute-start | bytes 294920 | tf_op jit(solution)/shard_map/ppermute | solution.py:213
